TPU v7x, 32 devices: a whole 2x2x4 slice. The times are simulated.
32 devices in a mesh: grp: 2 (over x), dev: 16 (over z, y, core).
Axes of the slice: x: 2, y: 2, z: 4, core: 2. Of those that a mesh axis runs over, the one named last changes fastest.
Arguments:
- state: float32 [2, 3, 16777216], P('grp', None, 'dev'), may hold values from -6 to 6
- courant: float32 [16777216], P('dev'), may hold values from 0.25 to 1
- remesh: float32 [128, 128], replicated, may hold values from -0.5 to 0.5
- shell_dest: int32 [32768, 1], P('dev'), may hold values from 0 to 15; in each aligned block of 2048 rows (0 to 2047, 2048 to 4095, ...) at most 256 rows name the same one
- shell_row: int32 [32768], P('dev'), may hold values from 0 to 8191
- return_dest: int32 [32768, 1], P('dev'), may hold values from 0 to 15; in each aligned block of 2048 rows (0 to 2047, 2048 to 4095, ...) at most 256 rows name the same one
- return_row: int32 [32768], P('dev'), may hold values from 0 to 8191
- return_block: int32 [32768], P('dev'), may hold values from 0 to 127
Outputs:
- fields: float32 [2, 3, 16777216], P('grp', None, 'dev')
Inputs may be any that keep to these rules, and one draw needn't show every extreme that they name: `shell_dest`: among the rows of one device (2048 aligned rows) no brick is named more than 256 times, a bound that some block reaches. `return_dest`: among the rows of one brick (2048 aligned rows) no owner is named more than 256 times, a bound that some block reaches.
All inputs are finite; a program needn't handle non-finite values.
Results may differ from a plain program's by a relative error of at most 0.00027.
Values sent between devices are 32-bit elements; how exact they have to be, the bound alone decides.
A program may use at most 192 MiB of HBM per device.

v0:
```python
import functools

import jax
import jax.numpy as jnp
import ml_dtypes
import numpy as np
from jax import lax
from jax.experimental import pallas as pl
from jax.experimental.pallas import tpu as pltpu
from jax.sharding import PartitionSpec as P

NX = 512
NY = 256
NI = 64

viscosity = 0.2
coupling = 1.0

VMEM = pl.BlockSpec(memory_space=pltpu.VMEM)
SMEM = pl.BlockSpec(memory_space=pltpu.SMEM)
HBM = pl.BlockSpec(memory_space=pl.ANY)
ROOM = pltpu.CompilerParams(vmem_limit_bytes=56 * 1024 * 1024)


def sine_table(length):
    counts = np.arange(length, dtype=np.int64) + 1
    phase = counts[:, None] * counts[None, :] % (2 * (length + 1))
    table = np.sin(np.pi * phase / (length + 1)).astype(np.float32)
    high = table.astype(ml_dtypes.bfloat16)
    low = (table - high.astype(np.float32)).astype(ml_dtypes.bfloat16)
    return np.stack([high, low])


def laplace_eigen(length):
    counts = np.arange(length, dtype=np.float64) + 1.0
    return 4.0 * np.sin(0.5 * np.pi * counts / (length + 1)) ** 2


def split(value):
    high = value.astype(jnp.bfloat16)
    return high, (value - high.astype(jnp.float32)).astype(jnp.bfloat16)


def dot_pairs(left, right):
    dot = functools.partial(jnp.dot, preferred_element_type=jnp.float32)
    return dot(left[0], right[0]) + (dot(left[0], right[1]) + dot(left[1], right[0]))


def power(base, exponent):
    result = None
    while exponent:
        if exponent & 1:
            result = base if result is None else result * base
        exponent >>= 1
        if exponent:
            base = base * base
    return result


def move(source, target, sem):
    copy = pltpu.make_async_copy(source, target, sem)
    copy.start()
    return copy


def loop(count, body):
    lax.fori_loop(0, count, lambda i, _: (body(i), 0)[1], 0)


def unrolled(count, width, body):
    while count % width:
        width //= 2

    def several(i):
        for t in range(width):
            body(i * width + t)

    loop(count // width, several)


def index_kernel(cap, stride, bricks, dest_a, tag_a, dest_b, tag_b, slot_a, slot_b, out):
    def clear(b):
        out[(2 * b) * stride + cap] = 0
        out[(2 * b + 1) * stride + cap] = 0

    loop(bricks, clear)

    def place(q):
        for side, (dest, tag, slot) in enumerate(((dest_a, tag_a, slot_a), (dest_b, tag_b, slot_b))):
            brick = dest[q]
            base = (2 * brick + side) * stride
            rank = out[base + cap]
            out[base + cap] = rank + 1
            slot[q] = brick * (3 * cap) + rank
            out[base + rank] = tag[q]

    unrolled(dest_a.shape[0], 8, place)


def pack_kernel(cap, group, slot, rows, out):
    @pl.when(lax.axis_index("grp") == group)
    def _():
        def place(i):
            first = pl.multiple_of(i * 8, 8)
            slots = [slot[first + t] for t in range(8)]
            for c in range(3):
                tile = rows[c, pl.ds(first, 8), :]
                for t in range(8):
                    out[pl.ds(slots[t] + c * cap, 1), :] = tile[t : t + 1, :]

        loop(rows.shape[1] // 8, place)


def accumulate(cap, stride, side, bricks, index, arrived, total):
    def from_brick(b):
        base = (2 * b + side) * stride

        def add(k):
            row = index[base + k]
            first = b * (3 * cap) + k
            news = [arrived[pl.ds(first + c * cap, 1), :] for c in range(3)]
            olds = [total[c, pl.ds(row, 1), :] for c in range(3)]
            for c in range(3):
                total[c, pl.ds(row, 1), :] = olds[c] + news[c]

        loop(index[base + cap], add)

    loop(bricks, from_brick)


def forward_kernel(
    cap, stride, bricks, index, arrived, field, decay, table_y, table_z, out, moments, held, sem
):
    planes = field.shape[1] // NY

    @pl.when(lax.axis_index("grp") == 1)
    def _():
        move(field, held, sem).wait()
        accumulate(cap, stride, 0, bricks, index, arrived, held)
        moments[...] = jnp.zeros_like(moments)
        r = decay[0]
        decay_now = (table_z[0], table_z[1])

        def plane(i):
            rows = pl.ds(pl.multiple_of(i * NY, NY), NY)
            parts = [dot_pairs(split(held[c, rows, :]), decay_now) for c in range(3)]
            wide = dot_pairs((table_y[0], table_y[1]), split(jnp.concatenate(parts, axis=1)))
            width = wide.shape[1] // 3
            for c in range(3):
                now = wide[:, c * width : (c + 1) * width]
                held[c, rows, :] = now
                moments[0, c] = now + r * moments[0, c]

        loop(planes, plane)
        sent = move(held, out, sem)

        def back(i):
            rows = pl.ds(pl.multiple_of((planes - 1 - i) * NY, NY), NY)
            for c in range(3):
                moments[1, c] = r * (held[c, rows, :] + moments[1, c])

        loop(planes, back)
        sent.wait()


def reduced_kernel(planes, moments, decay, out):
    bricks = moments.shape[0]
    r = decay[...]
    r_slab = power(r, planes)
    r_line = power(r, bricks * planes + 1)
    zero = jnp.zeros(moments.shape[2:], jnp.float32)

    def up(d, carry):
        out[d, 0] = carry
        return moments[d, 0] + r_slab * carry

    def down(i, carry):
        d = bricks - 1 - i
        out[d, 1] = carry
        return moments[d, 1] + r_slab * carry

    right = r * lax.fori_loop(0, bricks, up, zero)
    left = lax.fori_loop(0, bricks, down, zero)
    inverse = 1.0 / (1.0 - r_line * r_line)
    start = (right * r_line - left) * inverse
    end = (left * r_line - right) * inverse

    def add_up(d, carry):
        out[d, 0] += carry
        return r_slab * carry

    def add_down(i, carry):
        d = bricks - 1 - i
        out[d, 1] += carry
        return r_slab * carry

    lax.fori_loop(0, bricks, add_up, start)
    lax.fori_loop(0, bricks, add_down, r * end)


def backward_kernel(
    row, spectral, edges, decay, table_y, table_z, remesh_t, _fields, fields, interp, held, pot, run, sem
):
    planes = spectral.shape[1] // NY

    @pl.when(lax.axis_index("grp") == 1)
    def _():
        move(spectral, held, sem).wait()
        r = decay[0]
        gain = decay[1]
        run[...] = edges[...]

        def rows_of(i):
            return pl.ds(pl.multiple_of(i * NY, NY), NY)

        def potential(i, modes):
            wide = dot_pairs((table_y[0], table_y[1]), split(jnp.concatenate(modes, axis=1)))
            width = wide.shape[1] // 3
            for c in range(3):
                part = split(wide[:, c * width : (c + 1) * width])
                pot[c, rows_of(i), :] = dot_pairs(part, (table_z[0], table_z[1]))

        def back(i):
            at = planes - 1 - i
            for c in range(3):
                q = run[1, c]
                pot[c, rows_of(at + 1), :] = q
                run[1, c] = r * (held[c, rows_of(at), :] + q)

        loop(planes, back)
        potential(0, [gain * (run[0, c] + run[1, c]) for c in range(3)])

        def ahead(i):
            modes = []
            for c in range(3):
                p = held[c, rows_of(i), :] + r * run[0, c]
                run[0, c] = p
                modes.append(gain * (p + pot[c, rows_of(i + 1), :]))
            potential(i + 1, modes)

        loop(planes, ahead)
        potential(planes + 1, [gain * (r * run[0, c] + edges[1, c] / r) for c in range(3)])

        depth = pot.shape[2]
        y_at = lax.broadcasted_iota(jnp.int32, (NY, depth), 0)
        z_at = lax.broadcasted_iota(jnp.int32, (NY, depth), 1)

        def d_y(f):
            upper = jnp.where(y_at == NY - 1, 0.0, pltpu.roll(f, NY - 1, 0))
            return upper - jnp.where(y_at == 0, 0.0, pltpu.roll(f, 1, 0))

        def d_z(f):
            upper = jnp.where(z_at == depth - 1, 0.0, pltpu.roll(f, depth - 1, 1))
            return upper - jnp.where(z_at == 0, 0.0, pltpu.roll(f, 1, 1))

        def curl(i):
            here = rows_of(i + 1)
            f = [pot[c, here, :] for c in range(3)]
            slope_y = pot[1, rows_of(i + 2), :] - pot[1, rows_of(i), :]
            slope_z = pot[2, rows_of(i + 2), :] - pot[2, rows_of(i), :]
            held[0, rows_of(i), :] = 0.5 * (d_y(f[2]) - d_z(f[1]))
            held[1, rows_of(i), :] = 0.5 * (d_z(f[0]) - slope_z)
            held[2, rows_of(i), :] = 0.5 * (slope_y - d_y(f[0]))

        loop(planes, curl)
        sent = move(held, fields, sem)

        def pick(i):
            first = pl.multiple_of(i * 8, 8)
            places = [row[first + t] for t in range(8)]
            for c in range(3):
                for t in range(8):
                    interp[c, pl.ds(first + t, 1), :] = held[c, pl.ds(places[t], 1), :]

        loop(interp.shape[1] // 8, pick)
        weights = split(remesh_t[...])
        count = min(256, interp.shape[1])

        def project(i):
            rows = pl.ds(pl.multiple_of(i * count, count), count)
            for c in range(3):
                interp[c, rows, :] = dot_pairs(split(interp[c, rows, :]), weights)

        loop(interp.shape[1] // count, project)
        sent.wait()


def advance_kernel(near, courant, before, after, out, ext, first, sems):
    rows_j = near.shape[1]

    @pl.when(lax.axis_index("grp") == 0)
    def _():
        copies = [
            move(near, ext.at[pl.ds(0, 3), pl.ds(4, rows_j)], sems.at[0]),
            move(courant, ext.at[3, pl.ds(4, rows_j)], sems.at[1]),
            move(before, ext.at[:, pl.ds(0, 4)], sems.at[2]),
            move(after, ext.at[:, pl.ds(rows_j + 4, 4)], sems.at[3]),
        ]
        for copy in copies:
            copy.wait()
        i_at = lax.broadcasted_iota(jnp.int32, near.shape[2:], 0)

        def stepped(f, speed):
            transport = (8.0 * (f[3] - f[1]) - (f[4] - f[0])) * (1.0 / 12.0)
            upper = jnp.where(i_at == NI - 1, 0.0, pltpu.roll(f[2], NI - 1, 0))
            lower = jnp.where(i_at == 0, 0.0, pltpu.roll(f[2], 1, 0))
            return f[2] - speed * transport + viscosity * (upper - 2.0 * f[2] + lower)

        def one(j):
            speed = ext[3, j + 2]
            for c in range(3):
                first[c, j] = stepped([ext[c, j + t] for t in range(5)], speed)

        loop(rows_j + 4, one)

        def two(j):
            speed = ext[3, j + 4]
            for c in range(3):
                ext[c, j] = stepped([first[c, j + t] for t in range(5)], speed)

        loop(rows_j, two)
        move(ext.at[pl.ds(0, 3), pl.ds(0, rows_j)], out, sems.at[0]).wait()


def finish_kernel(cap, stride, bricks, index, arrived, layer, _fields, fields, boundary, rim, sem):
    @pl.when(lax.axis_index("grp") == 0)
    def _():
        fetched = move(fields.at[:, :, pl.ds(NI - 8, 8), :], rim, sem)
        boundary[...] = jnp.zeros_like(boundary)
        accumulate(cap, stride, 1, bricks, index, arrived, boundary)
        fetched.wait()
        for c in range(3):
            a, b = (c + 1) % 3, (c + 2) % 3
            turned = coupling * (boundary[a] * layer[b] - boundary[b] * layer[a])
            rim[c, :, 7, :] += turned
        move(rim, fields.at[:, :, pl.ds(NI - 8, 8), :], sem).wait()


def on_device(state, courant, remesh, shell_dest, shell_row, return_dest, return_row, return_block):
    bricks = lax.axis_size("dev")
    cell_count = state.shape[2]
    span_cells, lattice_z = remesh.shape
    rows_j = cell_count // (NI * span_cells)
    shell_depth = NI // 4
    shell_blocks = shell_depth * rows_j
    cap = 2 * shell_blocks // bricks
    stride = -(-(cap + 1) // 128) * 128
    planes = NX // bricks
    slab_rows = planes * NY
    f32 = functools.partial(jax.ShapeDtypeStruct, dtype=jnp.float32)
    i32 = functools.partial(jax.ShapeDtypeStruct, dtype=jnp.int32)
    field = state[0].reshape(3, slab_rows, lattice_z)
    near = field.reshape(3, rows_j, NI, span_cells)

    blocks = near[:, :, NI - shell_depth :, :].reshape(3, shell_blocks, span_cells)
    remeshed = jnp.einsum("cqk,kz->cqz", blocks, remesh, precision=lax.Precision.HIGH)
    crossed = lax.ppermute(remeshed, "grp", [(0, 1)])

    slot_shell, slot_back, tags = pl.pallas_call(
        functools.partial(index_kernel, cap, stride, bricks),
        out_shape=(i32((shell_blocks,)), i32((shell_blocks,)), i32((bricks * 2 * stride,))),
        in_specs=[SMEM] * 4,
        out_specs=(SMEM,) * 3,
    )(shell_dest[:, 0], shell_row, return_dest[:, 0], return_block)
    index = lax.all_to_all(
        tags.reshape(bricks, 2 * stride), "dev", split_axis=0, concat_axis=0, tiled=True
    ).reshape(-1)

    def exchange(rows, slots, group):
        packed = pl.pallas_call(
            functools.partial(pack_kernel, cap, group),
            out_shape=f32((bricks * 3 * cap, lattice_z)),
            in_specs=[SMEM, VMEM],
            out_specs=VMEM,
            compiler_params=ROOM,
        )(slots, rows)
        return lax.all_to_all(
            packed.reshape(bricks, 3 * cap, lattice_z),
            "dev",
            split_axis=0,
            concat_axis=0,
            tiled=True,
        ).reshape(bricks * 3 * cap, lattice_z)

    arrived = exchange(crossed, slot_shell, 1)

    table_y = sine_table(NY)
    table_z = sine_table(lattice_z)
    total = laplace_eigen(NY)[:, None] + laplace_eigen(lattice_z)[None, :]
    root = np.sqrt(total * (total + 4.0))
    decay = 2.0 / (2.0 + total + root)
    scale = 4.0 / ((NY + 1) * (lattice_z + 1))
    factors = jnp.asarray(np.stack([decay, scale / root]), jnp.float32)

    spectral, moments = pl.pallas_call(
        functools.partial(forward_kernel, cap, stride, bricks),
        out_shape=(f32((3, slab_rows, lattice_z)), f32((2, 3, NY, lattice_z))),
        in_specs=[SMEM, VMEM, HBM, VMEM, VMEM, VMEM],
        out_specs=(HBM, VMEM),
        scratch_shapes=[pltpu.VMEM((3, slab_rows, lattice_z), jnp.float32), pltpu.SemaphoreType.DMA],
        compiler_params=ROOM,
    )(index, arrived, field, factors, table_y, table_z)

    courant_near = courant.reshape(rows_j, NI, span_cells)
    ring_up = [(i, (i + 1) % bricks) for i in range(bricks)]
    ring_down = [(j, i) for i, j in ring_up]
    tail = jnp.concatenate([near[:, -4:], courant_near[None, -4:]], axis=0)
    head = jnp.concatenate([near[:, :4], courant_near[None, :4]], axis=0)
    before = lax.ppermute(tail, "dev", ring_up)
    after = lax.ppermute(head, "dev", ring_down)
    before, _ = lax.optimization_barrier((before, arrived))
    advanced = pl.pallas_call(
        advance_kernel,
        out_shape=f32((3, rows_j, NI, span_cells)),
        in_specs=[HBM] * 4,
        out_specs=HBM,
        scratch_shapes=[
            pltpu.VMEM((4, rows_j + 8, NI, span_cells), jnp.float32),
            pltpu.VMEM((3, rows_j + 4, NI, span_cells), jnp.float32),
            pltpu.SemaphoreType.DMA((4,)),
        ],
        compiler_params=ROOM,
    )(near, courant_near, before, after)

    lines = NY // bricks
    swapped = lax.all_to_all(
        moments.reshape(2, 3, bricks, lines, lattice_z).transpose(2, 0, 1, 3, 4),
        "dev",
        split_axis=0,
        concat_axis=0,
        tiled=True,
    )
    mine = lax.dynamic_slice_in_dim(factors[0], lax.axis_index("dev") * lines, lines)
    solved = pl.pallas_call(
        functools.partial(reduced_kernel, planes),
        out_shape=f32(swapped.shape),
        in_specs=[VMEM, VMEM],
        out_specs=VMEM,
    )(swapped, mine)
    edges = lax.all_to_all(solved, "dev", split_axis=0, concat_axis=0, tiled=True)
    edges = edges.transpose(1, 2, 0, 3, 4).reshape(2, 3, NY, lattice_z)

    fields, interp = pl.pallas_call(
        backward_kernel,
        out_shape=(f32((3, slab_rows, lattice_z)), f32((3, shell_blocks, span_cells))),
        in_specs=[SMEM, HBM, VMEM, VMEM, VMEM, VMEM, VMEM, HBM],
        out_specs=(HBM, VMEM),
        scratch_shapes=[
            pltpu.VMEM((3, slab_rows, lattice_z), jnp.float32),
            pltpu.VMEM((3, slab_rows + 2 * NY, lattice_z), jnp.float32),
            pltpu.VMEM((2, 3, NY, lattice_z), jnp.float32),
            pltpu.SemaphoreType.DMA,
        ],
        input_output_aliases={7: 0},
        compiler_params=ROOM,
    )(
        return_row,
        spectral,
        edges,
        factors,
        table_y,
        table_z,
        remesh.T,
        advanced.reshape(3, slab_rows, lattice_z),
    )

    returned = exchange(lax.ppermute(interp, "grp", [(1, 0)]), slot_back, 0)
    fields = pl.pallas_call(
        functools.partial(finish_kernel, cap, stride, bricks),
        out_shape=f32((3, rows_j, NI, span_cells)),
        in_specs=[SMEM, VMEM, VMEM, HBM],
        out_specs=HBM,
        scratch_shapes=[
            pltpu.VMEM((3, rows_j, span_cells), jnp.float32),
            pltpu.VMEM((3, rows_j, 8, span_cells), jnp.float32),
            pltpu.SemaphoreType.DMA,
        ],
        input_output_aliases={3: 0},
        compiler_params=ROOM,
    )(index, returned, near[:, :, NI - 1, :], fields.reshape(3, rows_j, NI, span_cells))
    return fields.reshape(1, 3, cell_count)


def solution(mesh):
    placed = (
        P("grp", None, "dev"),
        P("dev"),
        P(),
        P("dev", None),
        P("dev"),
        P("dev", None),
        P("dev"),
        P("dev"),
    )
    return jax.shard_map(
        on_device, mesh=mesh, in_specs=placed, out_specs=P("grp", None, "dev"), check_vma=False
    )
```

profile of v0, /device:TPU:21, one launch (start us, length us, event | category | flops | bytes accessed | tf_op | source)
XLA Modules:
  0.0 657.5 jit_solution(12591076069482800482)
XLA Ops:
  0.0 0.0 copy-start.5
  0.0 2.2 slice.52
  2.2 0.0 copy-done.5
  2.2 1.4 fusion
  3.6 4.8 collective-permute-start
  8.3 25.8 %shard_map.109 = (s32[2048]{0:T(1024)}, s32[2048]{0:T(1024)}, s32[12288]{0:T(1024)}) custom-call(s32[2048]{0:T(1024)} %bitcast.55, s32[2048]{0:T(1024)} %tag_a.1, s32[2048]{0:T(1024)} %bitcast.56, s32[2048]{0:T(1024)} %tag_b.1), custom_call_target="tpu_custom_call" | custom-call | tf_op jit(solution)/shard_map/pallas_call | solution.py:359
  34.1 6.7 %all-to-all-start = ((s32[16,1,768]{2,1,0:T(1,128)}), s32[16,1,768]{2,1,0:T(1,128)S(1)}, u32[]{:S(2)}, u32[]{:S(2)}) async-start(s32[16,1,768]{2,1,0:T(1,128)} %bitcast.54), calls=%async_computation | async-start | bytes 98304 | tf_op jit(solution)/shard_map/all_to_all | solution.py:365
  40.9 32.6 %collective-permute-done.rows = f32[3,2048,128]{2,1,0:T(8,128)} collective-permute-done((f32[3,2048,128]{2,1,0:T(8,128)S(1)}, f32[3,2048,128]{2,1,0:T(8,128)}, u32[]{:S(2)}, u32[]{:S(2)}) %collective-permute-start) | collective-permute-done | bytes 3145760 | tf_op jit(solution)/shard_map/ppermute | solution.py:357
  73.4 4.6 shard_map.110
  78.1 0.0 all-to-all-done
  78.1 0.0 copy-start.4
  78.1 143.3 %all_to_all.29 = f32[16,768,128]{2,1,0:T(8,128)} all-to-all(f32[16,768,128]{2,1,0:T(8,128)} %bitcast.40), channel_id=1, replica_groups=mesh['grp'=2,'dev'=16] {'dev'}, dimensions={0} | all-to-all | bytes 12582912 | tf_op jit(solution)/shard_map/all_to_all | solution.py:377
  221.4 0.0 copy-done.4
  221.4 3.8 shard_map.111
  225.2 2.2 copy.27
  227.4 6.8 %all-to-all-start.2 = ((f32[16,2,3,16,128]{4,3,2,1,0:T(8,128)}), f32[16,2,3,16,128]{4,3,2,1,0:T(8,128)S(1)}, u32[]{:S(2)}, u32[]{:S(2)}) async-start(f32[16,2,3,16,128]{4,3,2,1,0:T(8,128)} %bitcast.32), calls=%async_computation.2 | async-start | bytes 1572864 | tf_op jit(solution)/shard_map/all_to_all | solution.py:426
  234.2 1.3 dynamic-slice_bitcast_fusion.decay
  235.4 1.2 fusion.2
  236.6 14.8 %all-to-all-done.2.moments = f32[16,2,3,16,128]{4,3,2,1,0:T(8,128)S(1)} async-done(((f32[16,2,3,16,128]{4,3,2,1,0:T(8,128)}), f32[16,2,3,16,128]{4,3,2,1,0:T(8,128)S(1)}, u32[]{:S(2)}, u32[]{:S(2)}) %all-to-all-start.2) | async-done | bytes 786464 | tf_op jit(solution)/shard_map/all_to_all | solution.py:426
  251.4 0.0 copy-start
  251.4 0.9 copy-done
  252.3 2.5 shard_map.112
  254.7 6.9 %all-to-all-start.3 = ((f32[16,2,3,16,128]{4,3,2,1,0:T(8,128)}), f32[16,2,3,16,128]{4,3,2,1,0:T(8,128)S(1)}, u32[]{:S(2)}, u32[]{:S(2)}) async-start(f32[16,2,3,16,128]{4,3,2,1,0:T(8,128)} %shard_map.112), calls=%async_computation.3 | async-start | bytes 1572864 | tf_op jit(solution)/shard_map/all_to_all | solution.py:440
  261.7 1.0 fusion.3
  262.7 1.5 collective-permute-start.1
  264.3 0.1 collective-permute-start.2
  264.3 0.7 copy.22
  265.1 15.6 %collective-permute-done.1.before = f32[4,4,64,128]{3,2,1,0:T(8,128)S(1)} collective-permute-done((f32[4,4,64,128]{3,2,1,0:T(8,128)S(1)}, f32[4,4,64,128]{3,2,1,0:T(8,128)S(1)}, u32[]{:S(2)}, u32[]{:S(2)}) %collective-permute-start.1) | collective-permute-done | bytes 524320 | tf_op jit(solution)/shard_map/ppermute | solution.py:409
  280.7 0.0 copy-start.2
  280.7 2.1 collective-permute-done.2.after
  282.7 0.0 copy-start.3
  282.7 0.0 copy-done.2
  282.7 0.8 copy-done.3
  283.5 25.8 %shard_map.113 = f32[3,128,64,128]{3,2,1,0:T(8,128)} custom-call(f32[3,128,64,128]{3,2,1,0:T(8,128)} %bitcast.38, f32[128,64,128]{2,1,0:T(8,128)} %bitcast.44, f32[4,4,64,128]{3,2,1,0:T(8,128)} %copy-done.2, f32[4,4,64,128]{3,2,1,0:T(8,128)} %copy-done.3), custom_call_target="tpu_custom_call" | custom-call | tf_op jit(solution)/shard_map/pallas_call | solution.py:412
  309.3 0.0 all-to-all-done.3
  309.3 1.0 copy.21
  310.2 3.0 shard_map.114
  313.2 1.3 collective-permute-start.3
  314.5 156.5 %collective-permute-done.3.rows = f32[3,2048,128]{2,1,0:T(8,128)S(1)} collective-permute-done((f32[3,2048,128]{2,1,0:T(8,128)}, f32[3,2048,128]{2,1,0:T(8,128)S(1)}, u32[]{:S(2)}, u32[]{:S(2)}) %collective-permute-start.3) | collective-permute-done | bytes 3145760 | tf_op jit(solution)/shard_map/ppermute | solution.py:467
  471.1 0.0 copy-start.1
  471.1 1.7 copy-done.1
  472.8 9.0 %shard_map.115 = f32[12288,128]{1,0:T(8,128)} custom-call(s32[2048]{0:T(1024)} %get-tuple-element.14.slot, f32[3,2048,128]{2,1,0:T(8,128)} %copy-done.1), custom_call_target="tpu_custom_call" | custom-call | tf_op jit(solution)/shard_map/pallas_call | solution.py:370
  481.8 8.2 %all-to-all-start.4 = ((f32[16,768,128]{2,1,0:T(8,128)}), f32[16,768,128]{2,1,0:T(8,128)}, u32[]{:S(2)}, u32[]{:S(2)}) async-start(f32[16,768,128]{2,1,0:T(8,128)} %bitcast.41), calls=%async_computation.4 | async-start | bytes 12582912 | tf_op jit(solution)/shard_map/all_to_all | solution.py:377
  490.0 2.3 slice.55
  492.3 133.0 %all-to-all-done.4 = f32[16,768,128]{2,1,0:T(8,128)} async-done(((f32[16,768,128]{2,1,0:T(8,128)}), f32[16,768,128]{2,1,0:T(8,128)}, u32[]{:S(2)}, u32[]{:S(2)}) %all-to-all-start.4) | async-done | bytes 6291488 | tf_op jit(solution)/shard_map/all_to_all | solution.py:377
  625.3 32.2 %shard_map.116 = f32[3,128,64,128]{3,2,1,0:T(8,128)} custom-call(s32[12288]{0:T(1024)} %bitcast.52, f32[12288,128]{1,0:T(8,128)} %bitcast.21.arrived, f32[3,128,128]{2,1,0:T(8,128)} %bitcast.47, f32[3,128,64,128]{3,2,1,0:T(8,128)} %bitcast.34), custom_call_target="tpu_custom_call", output_to_operand_aliasing={{}: (3, {})} | custom-call | tf_op jit(solution)/shard_map/pallas_call | solution.py:468
  (2 shorter events, 0.1 us)
Async XLA Ops:
  0.0 2.2 copy-start.5
  3.6 69.9 %collective-permute-start = (f32[3,2048,128]{2,1,0:T(8,128)S(1)}, f32[3,2048,128]{2,1,0:T(8,128)}, u32[]{:S(2)}, u32[]{:S(2)}) collective-permute-start(f32[3,2048,128]{2,1,0:T(8,128)S(1)} %fusion), channel_id=1, source_target_pairs={{0,16},{1,17},{2,18},{3,19},{4,20},{5,21},{6,22},{7,23},{8,24},{9,... | collective-permute-start | bytes 9437192 | tf_op jit(solution)/shard_map/ppermute | solution.py:357
  34.1 43.9 %all-to-all-start = ((s32[16,1,768]{2,1,0:T(1,128)}), s32[16,1,768]{2,1,0:T(1,128)S(1)}, u32[]{:S(2)}, u32[]{:S(2)}) async-start(s32[16,1,768]{2,1,0:T(1,128)} %bitcast.54), calls=%async_computation | async-start | bytes 98304 | tf_op jit(solution)/shard_map/all_to_all | solution.py:365
  78.1 143.3 %copy-start.4 = (s32[16,1,768]{2,1,0:T(1,128)}, s32[16,1,768]{2,1,0:T(1,128)S(1)}, u32[]{:S(2)}) copy-start(s32[16,1,768]{2,1,0:T(1,128)S(1)} %all-to-all-done) | copy-start | bytes 147460
  227.4 24.0 %all-to-all-start.2 = ((f32[16,2,3,16,128]{4,3,2,1,0:T(8,128)}), f32[16,2,3,16,128]{4,3,2,1,0:T(8,128)S(1)}, u32[]{:S(2)}, u32[]{:S(2)}) async-start(f32[16,2,3,16,128]{4,3,2,1,0:T(8,128)} %bitcast.32), calls=%async_computation.2 | async-start | bytes 1572864 | tf_op jit(solution)/shard_map/all_to_all | solution.py:426
  251.4 0.9 copy-start
  254.7 54.5 %all-to-all-start.3 = ((f32[16,2,3,16,128]{4,3,2,1,0:T(8,128)}), f32[16,2,3,16,128]{4,3,2,1,0:T(8,128)S(1)}, u32[]{:S(2)}, u32[]{:S(2)}) async-start(f32[16,2,3,16,128]{4,3,2,1,0:T(8,128)} %shard_map.112), calls=%async_computation.3 | async-start | bytes 1572864 | tf_op jit(solution)/shard_map/all_to_all | solution.py:440
  262.7 17.9 %collective-permute-start.1 = (f32[4,4,64,128]{3,2,1,0:T(8,128)S(1)}, f32[4,4,64,128]{3,2,1,0:T(8,128)S(1)}, u32[]{:S(2)}, u32[]{:S(2)}) collective-permute-start(f32[4,4,64,128]{3,2,1,0:T(8,128)S(1)} %pad_maximum_fusion), channel_id=1, source_target_pairs={{0,1},{1,2},{2,3},{3,4},{4,5},{5,6},{6,7},{7,8},{8,9},{9,10},{10,1... | collective-permute-start | bytes 1572872 | tf_op jit(solution)/shard_map/ppermute | solution.py:409
  264.3 18.5 %collective-permute-start.2 = (f32[4,4,64,128]{3,2,1,0:T(8,128)S(1)}, f32[4,4,64,128]{3,2,1,0:T(8,128)S(1)}, u32[]{:S(2)}, u32[]{:S(2)}) collective-permute-start(f32[4,4,64,128]{3,2,1,0:T(8,128)S(1)} %pad_maximum_fusion.1), channel_id=1, source_target_pairs={{1,0},{2,1},{3,2},{4,3},{5,4},{6,5},{7,6},{8,7},{9,8},{10,9},{11,1... | collective-permute-start | bytes 1572872 | tf_op jit(solution)/shard_map/ppermute | solution.py:410
  280.7 2.1 copy-start.2
  282.7 0.8 copy-start.3
  313.2 157.8 %collective-permute-start.3 = (f32[3,2048,128]{2,1,0:T(8,128)}, f32[3,2048,128]{2,1,0:T(8,128)S(1)}, u32[]{:S(2)}, u32[]{:S(2)}) collective-permute-start(f32[3,2048,128]{2,1,0:T(8,128)} %get-tuple-element.19), channel_id=1, source_target_pairs={{16,0},{17,1},{18,2},{19,3},{20,4},{21,5},{22,6},{23,7},{24,8},{25... | collective-permute-start | bytes 9437192 | tf_op jit(solution)/shard_map/ppermute | solution.py:467
  471.1 1.7 copy-start.1
  481.8 143.5 %all-to-all-start.4 = ((f32[16,768,128]{2,1,0:T(8,128)}), f32[16,768,128]{2,1,0:T(8,128)}, u32[]{:S(2)}, u32[]{:S(2)}) async-start(f32[16,768,128]{2,1,0:T(8,128)} %bitcast.41), calls=%async_computation.4 | async-start | bytes 12582912 | tf_op jit(solution)/shard_map/all_to_all | solution.py:377
where the time goes:
time: 661 us; the launch traced here: 657 us
  waiting for transfers between devices  355 us (54%)
  blocking collectives  143 us (22%)
  Pallas kernels  107 us (16%)
  starting transfers between devices  36.3 us (5%)
  local copies, waits for them, and re-layouts  15.1 us (2%)
    ppermute x1, waiting for transfers between devices, on_device(): returned = exchange(lax.ppermute(interp, 'grp', [(1, 0)]), slot_back, 0)  157 us
    all_to_all x1, blocking collectives, exchange(): lax.all_to_all(packed.reshape(bricks, 3 * cap, lattice_z), 'dev', split_a...  143 us
    all_to_all x1, waiting for transfers between devices, exchange(): lax.all_to_all(packed.reshape(bricks, 3 * cap, lattice_z), 'dev', split_a...  133 us
    ppermute x1, waiting for transfers between devices, on_device(): crossed = lax.ppermute(remeshed, 'grp', [(0, 1)])  32.6 us
    pallas_call x1, Pallas kernels, on_device(): pl.pallas_call(functools.partial(finish_kernel, cap, stride, bricks), out...  32.2 us
    pallas_call x1, Pallas kernels, on_device(): pl.pallas_call(functools.partial(index_kernel, cap, stride, bricks), out_...  25.8 us
    pallas_call x1, Pallas kernels, on_device(): pl.pallas_call(advance_kernel, out_shape=f32((3, rows_j, NI, span_cells))...  25.8 us
    ppermute x1, waiting for transfers between devices, on_device(): before = lax.ppermute(tail, 'dev', ring_up)  15.6 us
  transfers between devices with their start and end apart: 8, of which 6 were waited for; matrix products, arithmetic and copies ran while one was open for 1% of the time, Pallas kernels for 9%

commit v1 on v0

--- a/solution.py
+++ b/solution.py
@@ -44,6 +44,19 @@
 def dot_pairs(left, right):
     dot = functools.partial(jnp.dot, preferred_element_type=jnp.float32)
     return dot(left[0], right[0]) + (dot(left[0], right[1]) + dot(left[1], right[0]))
+
+
+def doubled(pair):
+    wide = jnp.concatenate(pair, axis=1)
+    return jnp.concatenate([wide, wide], axis=0)
+
+
+def dot_doubled(left, right):
+    product = jnp.dot(
+        jnp.concatenate(split(left), axis=1), right, preferred_element_type=jnp.float32
+    )
+    width = product.shape[1] // 2
+    return product[:, :width] + product[:, width:]
 
 
 def power(base, exponent):
@@ -78,23 +91,84 @@
     loop(count // width, several)
 
 
-def index_kernel(cap, stride, bricks, dest_a, tag_a, dest_b, tag_b, slot_a, slot_b, out):
+def index_kernel(cap, stride, bricks, dest_a, tag_a, dest_b, tag_b, slot_a, slot_b, out_a, out_b):
+    half = dest_a.shape[0] // 2
+
     def clear(b):
-        out[(2 * b) * stride + cap] = 0
-        out[(2 * b + 1) * stride + cap] = 0
+        for out in (out_a, out_b):
+            for end in range(2):
+                out[b * stride + cap + end] = 0
 
     loop(bricks, clear)
+    sides = ((dest_a, tag_a, slot_a, out_a), (dest_b, tag_b, slot_b, out_b))
+    chains = [(side, end) for side in range(2) for end in range(2)]
 
     def place(q):
-        for side, (dest, tag, slot) in enumerate(((dest_a, tag_a, slot_a), (dest_b, tag_b, slot_b))):
-            brick = dest[q]
-            base = (2 * brick + side) * stride
-            rank = out[base + cap]
-            out[base + cap] = rank + 1
-            slot[q] = brick * (3 * cap) + rank
-            out[base + rank] = tag[q]
-
-    unrolled(dest_a.shape[0], 8, place)
+        at = [q + end * half for side, end in chains]
+        brick = [sides[side][0][at[n]] for n, (side, end) in enumerate(chains)]
+        tag = [sides[side][1][at[n]] for n, (side, end) in enumerate(chains)]
+        base = [value * stride for value in brick]
+        taken = [sides[side][3][base[n] + cap + end] for n, (side, end) in enumerate(chains)]
+        for n, (side, end) in enumerate(chains):
+            out = sides[side][3]
+            rank = cap - 1 - taken[n] if end else taken[n]
+            out[base[n] + cap + end] = taken[n] + 1
+            out[base[n] + rank] = tag[n]
+            sides[side][2][at[n]] = brick[n] * (3 * cap) + rank
+
+    unrolled(half, 4, place)
+
+
+def exchange_kernel(source, bricks, packed, tags, out, out_tags, send_sems, recv_sems):
+    grp = lax.axis_index("grp")
+    me = lax.axis_index("dev")
+    barrier = pltpu.get_barrier_semaphore()
+
+    def greet(i):
+        pl.semaphore_signal(
+            barrier,
+            inc=1,
+            device_id=(1 - grp, lax.rem(me + i, bricks)),
+            device_id_type=pl.DeviceIdType.MESH,
+        )
+
+    loop(bricks, greet)
+    pl.semaphore_wait(barrier, bricks)
+
+    def copies(block, place, peer):
+        return [
+            pltpu.make_async_remote_copy(
+                src_ref=source_ref.at[block],
+                dst_ref=target_ref.at[place],
+                send_sem=send_sems.at[n, block],
+                recv_sem=recv_sems.at[n, place],
+                device_id=(1 - grp, peer),
+                device_id_type=pl.DeviceIdType.MESH,
+            )
+            for n, (source_ref, target_ref) in enumerate(((packed, out), (tags, out_tags)))
+        ]
+
+    @pl.when(grp == source)
+    def _():
+        def start(i):
+            peer = lax.rem(me + i, bricks)
+            for copy in copies(peer, me, peer):
+                copy.start()
+
+        def finish(peer):
+            for copy in copies(peer, me, peer):
+                copy.wait_send()
+
+        loop(bricks, start)
+        loop(bricks, finish)
+
+    @pl.when(grp != source)
+    def _():
+        def finish(peer):
+            for copy in copies(peer, peer, peer):
+                copy.wait_recv()
+
+        loop(bricks, finish)
 
 
 def pack_kernel(cap, group, slot, rows, out):
@@ -111,9 +185,9 @@
         loop(rows.shape[1] // 8, place)
 
 
-def accumulate(cap, stride, side, bricks, index, arrived, total):
+def accumulate(cap, stride, bricks, index, arrived, total):
     def from_brick(b):
-        base = (2 * b + side) * stride
+        base = b * stride
 
         def add(k):
             row = index[base + k]
@@ -124,6 +198,8 @@
                 total[c, pl.ds(row, 1), :] = olds[c] + news[c]
 
         loop(index[base + cap], add)
+        last = cap - 1
+        loop(index[base + cap + 1], lambda k: add(last - k))
 
     loop(bricks, from_brick)
 
@@ -136,22 +212,28 @@
     @pl.when(lax.axis_index("grp") == 1)
     def _():
         move(field, held, sem).wait()
-        accumulate(cap, stride, 0, bricks, index, arrived, held)
+        accumulate(cap, stride, bricks, index, arrived, held)
         moments[...] = jnp.zeros_like(moments)
         r = decay[0]
-        decay_now = (table_z[0], table_z[1])
+        step = 2 - planes % 2
 
         def plane(i):
-            rows = pl.ds(pl.multiple_of(i * NY, NY), NY)
-            parts = [dot_pairs(split(held[c, rows, :]), decay_now) for c in range(3)]
+            first = i * (step * NY)
+            rows = pl.ds(pl.multiple_of(first, NY), step * NY)
+            parts = [dot_doubled(held[c, rows, :], table_z[...]) for c in range(3)]
+            parts = [part[t * NY : (t + 1) * NY] for t in range(step) for part in parts]
             wide = dot_pairs((table_y[0], table_y[1]), split(jnp.concatenate(parts, axis=1)))
-            width = wide.shape[1] // 3
-            for c in range(3):
-                now = wide[:, c * width : (c + 1) * width]
-                held[c, rows, :] = now
-                moments[0, c] = now + r * moments[0, c]
-
-        loop(planes, plane)
+            width = wide.shape[1] // (3 * step)
+            for c in range(3):
+                total = moments[0, c]
+                for t in range(step):
+                    n = 3 * t + c
+                    now = wide[:, n * width : (n + 1) * width]
+                    held[c, pl.ds(pl.multiple_of(first + t * NY, NY), NY), :] = now
+                    total = now + r * total
+                moments[0, c] = total
+
+        loop(planes // step, plane)
         sent = move(held, out, sem)
 
         def back(i):
@@ -213,12 +295,14 @@
         def rows_of(i):
             return pl.ds(pl.multiple_of(i * NY, NY), NY)
 
-        def potential(i, modes):
+        def potential(places, modes):
             wide = dot_pairs((table_y[0], table_y[1]), split(jnp.concatenate(modes, axis=1)))
-            width = wide.shape[1] // 3
-            for c in range(3):
-                part = split(wide[:, c * width : (c + 1) * width])
-                pot[c, rows_of(i), :] = dot_pairs(part, (table_z[0], table_z[1]))
+            width = wide.shape[1] // len(modes)
+            parts = [wide[:, n * width : (n + 1) * width] for n in range(len(modes))]
+            for c in range(3):
+                tall = dot_doubled(jnp.concatenate(parts[c::3], axis=0), table_z[...])
+                for t, place in enumerate(places):
+                    pot[c, rows_of(place), :] = tall[t * NY : (t + 1) * NY]
 
         def back(i):
             at = planes - 1 - i
@@ -228,18 +312,22 @@
                 run[1, c] = r * (held[c, rows_of(at), :] + q)
 
         loop(planes, back)
-        potential(0, [gain * (run[0, c] + run[1, c]) for c in range(3)])
+        step = 2 - planes % 2
 
         def ahead(i):
             modes = []
-            for c in range(3):
-                p = held[c, rows_of(i), :] + r * run[0, c]
-                run[0, c] = p
-                modes.append(gain * (p + pot[c, rows_of(i + 1), :]))
-            potential(i + 1, modes)
-
-        loop(planes, ahead)
-        potential(planes + 1, [gain * (r * run[0, c] + edges[1, c] / r) for c in range(3)])
+            for t in range(step):
+                at = i * step + t
+                for c in range(3):
+                    p = held[c, rows_of(at), :] + r * run[0, c]
+                    run[0, c] = p
+                    modes.append(gain * (p + pot[c, rows_of(at + 1), :]))
+            potential([i * step + t + 1 for t in range(step)], modes)
+
+        loop(planes // step, ahead)
+        below = [gain * (edges[0, c] + run[1, c]) for c in range(3)]
+        above = [gain * (r * run[0, c] + edges[1, c] / r) for c in range(3)]
+        potential([0, planes + 1], below + above)
 
         depth = pot.shape[2]
         y_at = lax.broadcasted_iota(jnp.int32, (NY, depth), 0)
@@ -273,13 +361,13 @@
                     interp[c, pl.ds(first + t, 1), :] = held[c, pl.ds(places[t], 1), :]
 
         loop(interp.shape[1] // 8, pick)
-        weights = split(remesh_t[...])
+        weights = doubled(split(remesh_t[...]))
         count = min(256, interp.shape[1])
 
         def project(i):
             rows = pl.ds(pl.multiple_of(i * count, count), count)
             for c in range(3):
-                interp[c, rows, :] = dot_pairs(split(interp[c, rows, :]), weights)
+                interp[c, rows, :] = dot_doubled(interp[c, rows, :], weights)
 
         loop(interp.shape[1] // count, project)
         sent.wait()
@@ -327,7 +415,7 @@
     def _():
         fetched = move(fields.at[:, :, pl.ds(NI - 8, 8), :], rim, sem)
         boundary[...] = jnp.zeros_like(boundary)
-        accumulate(cap, stride, 1, bricks, index, arrived, boundary)
+        accumulate(cap, stride, bricks, index, arrived, boundary)
         fetched.wait()
         for c in range(3):
             a, b = (c + 1) % 3, (c + 2) % 3
@@ -344,7 +432,7 @@
     shell_depth = NI // 4
     shell_blocks = shell_depth * rows_j
     cap = 2 * shell_blocks // bricks
-    stride = -(-(cap + 1) // 128) * 128
+    stride = -(-(cap + 2) // 128) * 128
     planes = NX // bricks
     slab_rows = planes * NY
     f32 = functools.partial(jax.ShapeDtypeStruct, dtype=jnp.float32)
@@ -354,38 +442,48 @@
 
     blocks = near[:, :, NI - shell_depth :, :].reshape(3, shell_blocks, span_cells)
     remeshed = jnp.einsum("cqk,kz->cqz", blocks, remesh, precision=lax.Precision.HIGH)
-    crossed = lax.ppermute(remeshed, "grp", [(0, 1)])
-
-    slot_shell, slot_back, tags = pl.pallas_call(
+
+    courant_near = courant.reshape(rows_j, NI, span_cells)
+    ring_up = [(i, (i + 1) % bricks) for i in range(bricks)]
+    ring_down = [(j, i) for i, j in ring_up]
+    tail = jnp.concatenate([near[:, -4:], courant_near[None, -4:]], axis=0)
+    head = jnp.concatenate([near[:, :4], courant_near[None, :4]], axis=0)
+    before = lax.ppermute(tail, "dev", ring_up)
+    after = lax.ppermute(head, "dev", ring_down)
+
+    slot_shell, slot_back, tags_shell, tags_back = pl.pallas_call(
         functools.partial(index_kernel, cap, stride, bricks),
-        out_shape=(i32((shell_blocks,)), i32((shell_blocks,)), i32((bricks * 2 * stride,))),
+        out_shape=(i32((shell_blocks,)), i32((shell_blocks,)), i32((bricks * stride,)), i32((bricks * stride,))),
         in_specs=[SMEM] * 4,
-        out_specs=(SMEM,) * 3,
+        out_specs=(SMEM,) * 4,
     )(shell_dest[:, 0], shell_row, return_dest[:, 0], return_block)
-    index = lax.all_to_all(
-        tags.reshape(bricks, 2 * stride), "dev", split_axis=0, concat_axis=0, tiled=True
-    ).reshape(-1)
-
-    def exchange(rows, slots, group):
-        packed = pl.pallas_call(
+    def pack(rows, slots, group):
+        return pl.pallas_call(
             functools.partial(pack_kernel, cap, group),
             out_shape=f32((bricks * 3 * cap, lattice_z)),
             in_specs=[SMEM, VMEM],
             out_specs=VMEM,
             compiler_params=ROOM,
-        )(slots, rows)
-        return lax.all_to_all(
-            packed.reshape(bricks, 3 * cap, lattice_z),
-            "dev",
-            split_axis=0,
-            concat_axis=0,
-            tiled=True,
-        ).reshape(bricks * 3 * cap, lattice_z)
-
-    arrived = exchange(crossed, slot_shell, 1)
+        )(slots, rows).reshape(bricks, 3 * cap, lattice_z)
+
+    def exchange(packed, tags, group):
+        arrived, index = pl.pallas_call(
+            functools.partial(exchange_kernel, group, bricks),
+            out_shape=(f32((bricks, 3 * cap, lattice_z)), i32((bricks, stride // 128, 128))),
+            in_specs=[HBM] * 2,
+            out_specs=(HBM,) * 2,
+            scratch_shapes=[pltpu.SemaphoreType.DMA((2, bricks))] * 2,
+            compiler_params=pltpu.CompilerParams(collective_id=group, has_side_effects=True),
+        )(packed, tags.reshape(bricks, stride // 128, 128))
+        return arrived.reshape(bricks * 3 * cap, lattice_z), index.reshape(-1)
+
+    packed = pack(remeshed, slot_shell, 0)
+    packed, before, after = lax.optimization_barrier((packed, before, after))
+    arrived, index = exchange(packed, tags_shell, 0)
+    before, _ = lax.optimization_barrier((before, arrived))
 
     table_y = sine_table(NY)
-    table_z = sine_table(lattice_z)
+    table_z = np.tile(np.concatenate(list(sine_table(lattice_z)), axis=1), (2, 1))
     total = laplace_eigen(NY)[:, None] + laplace_eigen(lattice_z)[None, :]
     root = np.sqrt(total * (total + 4.0))
     decay = 2.0 / (2.0 + total + root)
@@ -401,14 +499,6 @@
         compiler_params=ROOM,
     )(index, arrived, field, factors, table_y, table_z)
 
-    courant_near = courant.reshape(rows_j, NI, span_cells)
-    ring_up = [(i, (i + 1) % bricks) for i in range(bricks)]
-    ring_down = [(j, i) for i, j in ring_up]
-    tail = jnp.concatenate([near[:, -4:], courant_near[None, -4:]], axis=0)
-    head = jnp.concatenate([near[:, :4], courant_near[None, :4]], axis=0)
-    before = lax.ppermute(tail, "dev", ring_up)
-    after = lax.ppermute(head, "dev", ring_down)
-    before, _ = lax.optimization_barrier((before, arrived))
     advanced = pl.pallas_call(
         advance_kernel,
         out_shape=f32((3, rows_j, NI, span_cells)),
@@ -464,7 +554,7 @@
         advanced.reshape(3, slab_rows, lattice_z),
     )
 
-    returned = exchange(lax.ppermute(interp, "grp", [(1, 0)]), slot_back, 0)
+    returned, index_back = exchange(pack(interp, slot_back, 1), tags_back, 1)
     fields = pl.pallas_call(
         functools.partial(finish_kernel, cap, stride, bricks),
         out_shape=f32((3, rows_j, NI, span_cells)),
@@ -477,7 +567,7 @@
         ],
         input_output_aliases={3: 0},
         compiler_params=ROOM,
-    )(index, returned, near[:, :, NI - 1, :], fields.reshape(3, rows_j, NI, span_cells))
+    )(index_back, returned, near[:, :, NI - 1, :], fields.reshape(3, rows_j, NI, span_cells))
     return fields.reshape(1, 3, cell_count)
 
 

time: 661 us -> 518 us (0.78)
  Pallas kernels: 107 us -> 464 us
  waiting for transfers between devices: 355 us -> 16 us
  blocking collectives: 143 us -> 0 us
  starting transfers between devices: 36.3 us -> 14.3 us
    pallas_call x2 -> x4, Pallas kernels: 13.6 us -> 373 us  [the longest x2 359 us: exchange(): pl.pallas_call(functools.partial(exchange_kernel, group, bricks), out_sha...]
    ppermute x2 -> x0, waiting for transfers between devices: 189 us -> none  [the longest x1 157 us: on_device(): returned = exchange(lax.ppermute(interp, 'grp', [(1, 0)]), slot_back, 0)]
    all_to_all x1 -> x0, blocking collectives: 143 us -> none  [exchange(): lax.all_to_all(packed.reshape(bricks, 3 * cap, lattice_z), 'dev', split_a...]
    all_to_all x2 -> x0, waiting for transfers between devices: 133 us -> none  [the longest x1 133 us: exchange(): lax.all_to_all(packed.reshape(bricks, 3 * cap, lattice_z), 'dev', split_a...]
    ppermute x1, waiting for transfers between devices: 15.6 us -> 0.01 us  [on_device(): before = lax.ppermute(tail, 'dev', ring_up)]
    all_to_all x2 -> x0, starting transfers between devices: 14.9 us -> none  [the longest x1 8.2 us: exchange(): lax.all_to_all(packed.reshape(bricks, 3 * cap, lattice_z), 'dev', split_a...]
  transfers between devices with their start and end apart: 8 -> 4, of which waited for: 6 -> 1; matrix products, arithmetic and copies ran while one was open for 1% -> 2% of each run, Pallas kernels for 9% -> 11%
where the time goes in v1:
time: 518 us; the launch traced here: 517 us
  Pallas kernels  464 us (90%)
  local copies, waits for them, and re-layouts  17.3 us (3%)
  waiting for transfers between devices  16 us (3%)
  starting transfers between devices  14.3 us (3%)
    pallas_call x2, Pallas kernels, exchange(): pl.pallas_call(functools.partial(exchange_kernel, group, bricks), out_sha...  359 us
    pallas_call x1, Pallas kernels, on_device(): pl.pallas_call(functools.partial(finish_kernel, cap, stride, bricks), out...  32.7 us
    pallas_call x1, Pallas kernels, on_device(): pl.pallas_call(advance_kernel, out_shape=f32((3, rows_j, NI, span_cells))...  25.8 us
    pallas_call x1, Pallas kernels, on_device(): pl.pallas_call(functools.partial(index_kernel, cap, stride, bricks), out_...  24.1 us
    all_to_all x1, waiting for transfers between devices, on_device(): lax.all_to_all(moments.reshape(2, 3, bricks, lines, lattice_z).transpose(...  16 us
    pallas_call x2, Pallas kernels, pack(): pl.pallas_call(functools.partial(pack_kernel, cap, group), out_shape=f32(...  13.6 us
  transfers between devices with their start and end apart: 4, of which 1 were waited for; matrix products, arithmetic and copies ran while one was open for 2% of the time, Pallas kernels for 11%

profile of v1, /device:TPU:21, one launch (start us, length us, event | category | flops | bytes accessed | tf_op | source)
XLA Modules:
  0.0 516.8 jit_solution(15734765676003251462)
XLA Ops:
  0.0 0.0 copy-start.1
  0.0 1.2 fusion.2
  1.2 1.0 fusion.3
  2.2 0.8 pad_maximum_fusion
  3.0 1.8 collective-permute-start
  4.8 0.8 pad_maximum_fusion.1
  5.7 0.0 collective-permute-start.1
  5.7 2.1 slice.52
  7.8 24.1 %shard_map.109 = (s32[2048]{0:T(1024)}, s32[2048]{0:T(1024)}, s32[6144]{0:T(1024)}, s32[6144]{0:T(1024)}) custom-call(s32[2048]{0:T(1024)} %bitcast.51, s32[2048]{0:T(1024)} %tag_a.1, s32[2048]{0:T(1024)} %bitcast.52, s32[2048]{0:T(1024)} %tag_b.1), custom_call_target="tpu_custom_call" | custom-call | tf_op jit(solution)/shard_map/pallas_call | solution.py:454
  31.9 1.4 reshape.68.tags
  33.2 0.0 copy-done.1
  33.2 3.0 fusion.rows
  36.3 9.1 %shard_map.110 = f32[12288,128]{1,0:T(8,128)} custom-call(s32[2048]{0:T(1024)} %get-tuple-element.22.slot, f32[3,2048,128]{2,1,0:T(8,128)} %fusion.rows), custom_call_target="tpu_custom_call" | custom-call | tf_op jit(solution)/shard_map/pallas_call | solution.py:461
  45.3 0.0 collective-permute-done.before
  45.3 0.0 collective-permute-done.1.after
  45.3 136.9 %shard_map.111 = (f32[16,768,128]{2,1,0:T(8,128)}, s32[16,3,128]{2,1,0:T(4,128)}) custom-call(f32[16,768,128]{2,1,0:T(8,128)} %bitcast.38, s32[16,3,128]{2,1,0:T(4,128)} %reshape.68.tags), custom_call_target="tpu_custom_call" | custom-call | tf_op jit(solution)/shard_map/pallas_call | solution.py:470
  182.2 1.4 reshape.69.index
  183.6 3.8 shard_map.112
  187.4 0.0 copy-start.2
  187.4 2.2 copy.27
  189.6 5.5 %all-to-all-start = ((f32[16,2,3,16,128]{4,3,2,1,0:T(8,128)}), f32[16,2,3,16,128]{4,3,2,1,0:T(8,128)S(1)}, u32[]{:S(2)}, u32[]{:S(2)}) async-start(f32[16,2,3,16,128]{4,3,2,1,0:T(8,128)} %bitcast.30), calls=%async_computation | async-start | bytes 1572864 | tf_op jit(solution)/shard_map/all_to_all | solution.py:516
  195.1 1.3 dynamic-slice_bitcast_fusion.decay
  196.4 16.0 %all-to-all-done.moments = f32[16,2,3,16,128]{4,3,2,1,0:T(8,128)S(1)} async-done(((f32[16,2,3,16,128]{4,3,2,1,0:T(8,128)}), f32[16,2,3,16,128]{4,3,2,1,0:T(8,128)S(1)}, u32[]{:S(2)}, u32[]{:S(2)}) %all-to-all-start) | async-done | bytes 786464 | tf_op jit(solution)/shard_map/all_to_all | solution.py:516
  212.3 0.0 copy-start
  212.3 0.9 copy-done
  213.2 2.5 shard_map.113
  215.7 6.9 %all-to-all-start.1 = ((f32[16,2,3,16,128]{4,3,2,1,0:T(8,128)}), f32[16,2,3,16,128]{4,3,2,1,0:T(8,128)S(1)}, u32[]{:S(2)}, u32[]{:S(2)}) async-start(f32[16,2,3,16,128]{4,3,2,1,0:T(8,128)} %shard_map.113), calls=%async_computation.1 | async-start | bytes 1572864 | tf_op jit(solution)/shard_map/all_to_all | solution.py:530
  222.6 0.7 copy.22
  223.4 2.2 slice.55
  225.6 0.0 copy-done.2
  225.6 0.6 reshape.76.tags
  226.2 25.8 %shard_map.114 = f32[3,128,64,128]{3,2,1,0:T(8,128)} custom-call(f32[3,128,64,128]{3,2,1,0:T(8,128)} %bitcast.37, f32[128,64,128]{2,1,0:T(8,128)} %bitcast.43, f32[4,4,64,128]{3,2,1,0:T(8,128)} %collective-permute-done.before, f32[4,4,64,128]{3,2,1,0:T(8,128)} %collective-permute-done.1.after), custom_call_target="tpu_custom_call" | custom-call | tf_op jit(solution)/shard_map/pallas_call | solution.py:502
  252.0 0.0 all-to-all-done.1
  252.0 1.0 copy.21
  253.0 3.0 shard_map.115
  256.0 4.6 shard_map.116
  260.6 222.1 %shard_map.117 = (f32[16,768,128]{2,1,0:T(8,128)}, s32[16,3,128]{2,1,0:T(4,128)}) custom-call(f32[16,768,128]{2,1,0:T(8,128)} %bitcast.39, s32[16,3,128]{2,1,0:T(4,128)} %reshape.76.tags), custom_call_target="tpu_custom_call" | custom-call | tf_op jit(solution)/shard_map/pallas_call | solution.py:470
  482.7 1.4 reshape.77.index
  484.1 32.7 %shard_map.118 = f32[3,128,64,128]{3,2,1,0:T(8,128)} custom-call(s32[6144]{0:T(1024)} %reshape.77.index, f32[12288,128]{1,0:T(8,128)} %bitcast.42, f32[3,128,128]{2,1,0:T(8,128)} %bitcast.46, f32[3,128,64,128]{3,2,1,0:T(8,128)} %bitcast.32), custom_call_target="tpu_custom_call", output_to_operand_aliasing={{}: (3, {})} | custom-call | tf_op jit(solution)/shard_map/pallas_call | solution.py:558
Async XLA Ops:
  0.0 33.2 %copy-start.1 = (f32[128,128]{1,0:T(8,128)S(1)}, f32[128,128]{1,0:T(8,128)}, u32[]{:S(2)}) copy-start(f32[128,128]{1,0:T(8,128)} %param.13) | copy-start | bytes 196612
  3.0 42.3 %collective-permute-start = (f32[4,4,64,128]{3,2,1,0:T(8,128)}, f32[4,4,64,128]{3,2,1,0:T(8,128)}, u32[]{:S(2)}, u32[]{:S(2)}) collective-permute-start(f32[4,4,64,128]{3,2,1,0:T(8,128)} %pad_maximum_fusion), channel_id=1, source_target_pairs={{0,1},{1,2},{2,3},{3,4},{4,5},{5,6},{6,7},{7,8},{8,9},{9,10},{10,1... | collective-permute-start | bytes 1572872 | tf_op jit(solution)/shard_map/ppermute | solution.py:451
  5.7 39.7 %collective-permute-start.1 = (f32[4,4,64,128]{3,2,1,0:T(8,128)}, f32[4,4,64,128]{3,2,1,0:T(8,128)}, u32[]{:S(2)}, u32[]{:S(2)}) collective-permute-start(f32[4,4,64,128]{3,2,1,0:T(8,128)} %pad_maximum_fusion.1), channel_id=1, source_target_pairs={{1,0},{2,1},{3,2},{4,3},{5,4},{6,5},{7,6},{8,7},{9,8},{10,9},{11,1... | collective-permute-start | bytes 1572872 | tf_op jit(solution)/shard_map/ppermute | solution.py:452
  187.4 38.2 %copy-start.2 = (s32[6144]{0:T(1024)S(1)}, s32[6144]{0:T(1024)}, u32[]{:S(2)}) copy-start(s32[6144]{0:T(1024)} %get-tuple-element.33) | copy-start | bytes 73732
  189.6 22.7 %all-to-all-start = ((f32[16,2,3,16,128]{4,3,2,1,0:T(8,128)}), f32[16,2,3,16,128]{4,3,2,1,0:T(8,128)S(1)}, u32[]{:S(2)}, u32[]{:S(2)}) async-start(f32[16,2,3,16,128]{4,3,2,1,0:T(8,128)} %bitcast.30), calls=%async_computation | async-start | bytes 1572864 | tf_op jit(solution)/shard_map/all_to_all | solution.py:516
  212.3 0.9 copy-start
  215.7 36.3 %all-to-all-start.1 = ((f32[16,2,3,16,128]{4,3,2,1,0:T(8,128)}), f32[16,2,3,16,128]{4,3,2,1,0:T(8,128)S(1)}, u32[]{:S(2)}, u32[]{:S(2)}) async-start(f32[16,2,3,16,128]{4,3,2,1,0:T(8,128)} %shard_map.113), calls=%async_computation.1 | async-start | bytes 1572864 | tf_op jit(solution)/shard_map/all_to_all | solution.py:530

commit v2 on v1

--- a/solution.py
+++ b/solution.py
@@ -91,35 +91,36 @@
     loop(count // width, several)
 
 
-def index_kernel(cap, stride, bricks, dest_a, tag_a, dest_b, tag_b, slot_a, slot_b, out_a, out_b):
-    half = dest_a.shape[0] // 2
+def index_kernel(cap, stride, bricks, dest, tag, slot, out):
+    half = dest.shape[0] // 2
 
     def clear(b):
-        for out in (out_a, out_b):
-            for end in range(2):
-                out[b * stride + cap + end] = 0
+        for end in range(2):
+            out[b * stride + cap + end] = 0
 
     loop(bricks, clear)
-    sides = ((dest_a, tag_a, slot_a, out_a), (dest_b, tag_b, slot_b, out_b))
-    chains = [(side, end) for side in range(2) for end in range(2)]
 
     def place(q):
-        at = [q + end * half for side, end in chains]
-        brick = [sides[side][0][at[n]] for n, (side, end) in enumerate(chains)]
-        tag = [sides[side][1][at[n]] for n, (side, end) in enumerate(chains)]
+        at = [q, q + half]
+        brick = [dest[n] for n in at]
+        label = [tag[n] for n in at]
         base = [value * stride for value in brick]
-        taken = [sides[side][3][base[n] + cap + end] for n, (side, end) in enumerate(chains)]
-        for n, (side, end) in enumerate(chains):
-            out = sides[side][3]
-            rank = cap - 1 - taken[n] if end else taken[n]
-            out[base[n] + cap + end] = taken[n] + 1
-            out[base[n] + rank] = tag[n]
-            sides[side][2][at[n]] = brick[n] * (3 * cap) + rank
-
-    unrolled(half, 4, place)
-
-
-def exchange_kernel(source, bricks, packed, tags, out, out_tags, send_sems, recv_sems):
+        taken = [out[base[end] + cap + end] for end in range(2)]
+        for end in range(2):
+            rank = cap - 1 - taken[end] if end else taken[end]
+            out[base[end] + cap + end] = taken[end] + 1
+            out[base[end] + rank] = label[end]
+            slot[at[end]] = brick[end] * (3 * cap) + rank
+
+    unrolled(half, 8, place)
+
+
+def exchange_kernel(source, bricks, halo, *refs):
+    if halo:
+        packed, tags, near, courant, out, out_tags, before, after = refs[:8]
+        send_sems, recv_sems, rim_send, rim_recv = refs[8:]
+    else:
+        packed, tags, out, out_tags, send_sems, recv_sems = refs
     grp = lax.axis_index("grp")
     me = lax.axis_index("dev")
     barrier = pltpu.get_barrier_semaphore()
@@ -133,7 +134,42 @@
         )
 
     loop(bricks, greet)
-    pl.semaphore_wait(barrier, bricks)
+    neighbours = (lax.rem(me + 1, bricks), lax.rem(me + bricks - 1, bricks))
+
+    @pl.when(grp == source)
+    def _():
+        if halo:
+            for peer in neighbours:
+                pl.semaphore_signal(
+                    barrier, inc=1, device_id=(grp, peer), device_id_type=pl.DeviceIdType.MESH
+                )
+        pl.semaphore_wait(barrier, bricks + 2 if halo else bricks)
+
+    @pl.when(grp != source)
+    def _():
+        pl.semaphore_wait(barrier, bricks)
+
+    def rims():
+        if not halo:
+            return []
+        last = near.shape[1] - 4
+        pairs = (
+            (near.at[:, pl.ds(last, 4)], before.at[pl.ds(0, 3)]),
+            (courant.at[pl.ds(last, 4)], before.at[3]),
+            (near.at[:, pl.ds(0, 4)], after.at[pl.ds(0, 3)]),
+            (courant.at[pl.ds(0, 4)], after.at[3]),
+        )
+        return [
+            pltpu.make_async_remote_copy(
+                src_ref=source_ref,
+                dst_ref=target_ref,
+                send_sem=rim_send.at[n],
+                recv_sem=rim_recv.at[n],
+                device_id=(grp, neighbours[n // 2]),
+                device_id_type=pl.DeviceIdType.MESH,
+            )
+            for n, (source_ref, target_ref) in enumerate(pairs)
+        ]
 
     def copies(block, place, peer):
         return [
@@ -160,6 +196,10 @@
                 copy.wait_send()
 
         loop(bricks, start)
+        for copy in rims():
+            copy.start()
+        for copy in rims():
+            copy.wait()
         loop(bricks, finish)
 
     @pl.when(grp != source)
@@ -189,17 +229,22 @@
     def from_brick(b):
         base = b * stride
 
-        def add(k):
-            row = index[base + k]
-            first = b * (3 * cap) + k
-            news = [arrived[pl.ds(first + c * cap, 1), :] for c in range(3)]
-            olds = [total[c, pl.ds(row, 1), :] for c in range(3)]
-            for c in range(3):
-                total[c, pl.ds(row, 1), :] = olds[c] + news[c]
-
-        loop(index[base + cap], add)
-        last = cap - 1
-        loop(index[base + cap + 1], lambda k: add(last - k))
+        def add(places):
+            rows = [index[base + k] for k in places]
+            firsts = [b * (3 * cap) + k for k in places]
+            news = [[arrived[pl.ds(n + c * cap, 1), :] for c in range(3)] for n in firsts]
+            for row, new in zip(rows, news):
+                olds = [total[c, pl.ds(row, 1), :] for c in range(3)]
+                for c in range(3):
+                    total[c, pl.ds(row, 1), :] = olds[c] + new[c]
+
+        def several(count, place):
+            wide = count // 4
+            loop(wide, lambda i: add([place(4 * i + t) for t in range(4)]))
+            lax.fori_loop(4 * wide, count, lambda k, _: (add([place(k)]), 0)[1], 0)
+
+        several(index[base + cap], lambda k: k)
+        several(index[base + cap + 1], lambda k: cap - 1 - k)
 
     loop(bricks, from_brick)
 
@@ -245,39 +290,85 @@
         sent.wait()
 
 
-def reduced_kernel(planes, moments, decay, out):
-    bricks = moments.shape[0]
-    r = decay[...]
-    r_slab = power(r, planes)
-    r_line = power(r, bricks * planes + 1)
-    zero = jnp.zeros(moments.shape[2:], jnp.float32)
-
-    def up(d, carry):
-        out[d, 0] = carry
-        return moments[d, 0] + r_slab * carry
-
-    def down(i, carry):
-        d = bricks - 1 - i
-        out[d, 1] = carry
-        return moments[d, 1] + r_slab * carry
-
-    right = r * lax.fori_loop(0, bricks, up, zero)
-    left = lax.fori_loop(0, bricks, down, zero)
-    inverse = 1.0 / (1.0 - r_line * r_line)
-    start = (right * r_line - left) * inverse
-    end = (left * r_line - right) * inverse
-
-    def add_up(d, carry):
-        out[d, 0] += carry
-        return r_slab * carry
-
-    def add_down(i, carry):
-        d = bricks - 1 - i
-        out[d, 1] += carry
-        return r_slab * carry
-
-    lax.fori_loop(0, bricks, add_up, start)
-    lax.fori_loop(0, bricks, add_down, r * end)
+def reduced_kernel(planes, moments, decay, out, got, solved, send_sems, recv_sems, sem):
+    bricks = moments.shape[2]
+    grp = lax.axis_index("grp")
+    me = lax.axis_index("dev")
+
+    @pl.when(grp == 1)
+    def _():
+        barrier = pltpu.get_barrier_semaphore()
+
+        def greet(i):
+            pl.semaphore_signal(
+                barrier,
+                inc=1,
+                device_id=(grp, lax.rem(me + 1 + i, bricks)),
+                device_id_type=pl.DeviceIdType.MESH,
+            )
+
+        loop(bricks - 1, greet)
+        pl.semaphore_wait(barrier, bricks - 1)
+
+        def swap(n, source, target):
+            def copy(block, place, peer):
+                return pltpu.make_async_remote_copy(
+                    src_ref=source.at[:, :, block],
+                    dst_ref=target.at[:, :, place],
+                    send_sem=send_sems.at[n, block],
+                    recv_sem=recv_sems.at[n, place],
+                    device_id=(grp, peer),
+                    device_id_type=pl.DeviceIdType.MESH,
+                )
+
+            def start(i):
+                peer = lax.rem(me + 1 + i, bricks)
+                copy(peer, me, peer).start()
+
+            def finish(i):
+                peer = lax.rem(me + 1 + i, bricks)
+                copy(peer, me, peer).wait_send()
+                copy(peer, peer, peer).wait_recv()
+
+            loop(bricks - 1, start)
+            own = pltpu.make_async_copy(source.at[:, :, me], target.at[:, :, me], sem)
+            own.start()
+            own.wait()
+            loop(bricks - 1, finish)
+
+        swap(0, moments, got)
+        r = decay[...]
+        r_slab = power(r, planes)
+        r_line = power(r, bricks * planes + 1)
+        zero = jnp.zeros(got.shape[1:2] + got.shape[3:], jnp.float32)
+
+        def up(d, carry):
+            solved[0, :, d] = carry
+            return got[0, :, d] + r_slab * carry
+
+        def down(i, carry):
+            d = bricks - 1 - i
+            solved[1, :, d] = carry
+            return got[1, :, d] + r_slab * carry
+
+        right = r * lax.fori_loop(0, bricks, up, zero)
+        left = lax.fori_loop(0, bricks, down, zero)
+        inverse = 1.0 / (1.0 - r_line * r_line)
+        start_value = (right * r_line - left) * inverse
+        end_value = (left * r_line - right) * inverse
+
+        def add_up(d, carry):
+            solved[0, :, d] += carry
+            return r_slab * carry
+
+        def add_down(i, carry):
+            d = bricks - 1 - i
+            solved[1, :, d] += carry
+            return r_slab * carry
+
+        lax.fori_loop(0, bricks, add_up, start_value)
+        lax.fori_loop(0, bricks, add_down, r * end_value)
+        swap(1, solved, out)
 
 
 def backward_kernel(
@@ -444,19 +535,18 @@
     remeshed = jnp.einsum("cqk,kz->cqz", blocks, remesh, precision=lax.Precision.HIGH)
 
     courant_near = courant.reshape(rows_j, NI, span_cells)
-    ring_up = [(i, (i + 1) % bricks) for i in range(bricks)]
-    ring_down = [(j, i) for i, j in ring_up]
-    tail = jnp.concatenate([near[:, -4:], courant_near[None, -4:]], axis=0)
-    head = jnp.concatenate([near[:, :4], courant_near[None, :4]], axis=0)
-    before = lax.ppermute(tail, "dev", ring_up)
-    after = lax.ppermute(head, "dev", ring_down)
-
-    slot_shell, slot_back, tags_shell, tags_back = pl.pallas_call(
+    on_near = lax.axis_index("grp") == 0
+    slots, tags = pl.pallas_call(
         functools.partial(index_kernel, cap, stride, bricks),
-        out_shape=(i32((shell_blocks,)), i32((shell_blocks,)), i32((bricks * stride,)), i32((bricks * stride,))),
-        in_specs=[SMEM] * 4,
-        out_specs=(SMEM,) * 4,
-    )(shell_dest[:, 0], shell_row, return_dest[:, 0], return_block)
+        out_shape=(i32((shell_blocks,)), i32((bricks * stride,))),
+        in_specs=[SMEM] * 2,
+        out_specs=(SMEM,) * 2,
+    )(
+        jnp.where(on_near, shell_dest[:, 0], return_dest[:, 0]),
+        jnp.where(on_near, shell_row, return_block),
+    )
+    tags = tags.reshape(bricks, stride // 128, 128)
+
     def pack(rows, slots, group):
         return pl.pallas_call(
             functools.partial(pack_kernel, cap, group),
@@ -466,21 +556,25 @@
             compiler_params=ROOM,
         )(slots, rows).reshape(bricks, 3 * cap, lattice_z)
 
-    def exchange(packed, tags, group):
-        arrived, index = pl.pallas_call(
-            functools.partial(exchange_kernel, group, bricks),
-            out_shape=(f32((bricks, 3 * cap, lattice_z)), i32((bricks, stride // 128, 128))),
-            in_specs=[HBM] * 2,
-            out_specs=(HBM,) * 2,
-            scratch_shapes=[pltpu.SemaphoreType.DMA((2, bricks))] * 2,
+    def exchange(packed, group, *edge):
+        rim = f32((4, 4, NI, span_cells))
+        extra = 2 if edge else 0
+        arrived, index, *rims = pl.pallas_call(
+            functools.partial(exchange_kernel, group, bricks, bool(edge)),
+            out_shape=(
+                f32((bricks, 3 * cap, lattice_z)),
+                i32((bricks, stride // 128, 128)),
+                *[rim] * extra,
+            ),
+            in_specs=[HBM] * (2 + extra),
+            out_specs=(HBM,) * (2 + extra),
+            scratch_shapes=[pltpu.SemaphoreType.DMA((2, bricks))] * 2
+            + [pltpu.SemaphoreType.DMA((4,))] * extra,
             compiler_params=pltpu.CompilerParams(collective_id=group, has_side_effects=True),
-        )(packed, tags.reshape(bricks, stride // 128, 128))
-        return arrived.reshape(bricks * 3 * cap, lattice_z), index.reshape(-1)
-
-    packed = pack(remeshed, slot_shell, 0)
-    packed, before, after = lax.optimization_barrier((packed, before, after))
-    arrived, index = exchange(packed, tags_shell, 0)
-    before, _ = lax.optimization_barrier((before, arrived))
+        )(packed, tags, *edge)
+        return arrived.reshape(bricks * 3 * cap, lattice_z), index.reshape(-1), *rims
+
+    arrived, index, before, after = exchange(pack(remeshed, slots, 0), 0, near, courant_near)
 
     table_y = sine_table(NY)
     table_z = np.tile(np.concatenate(list(sine_table(lattice_z)), axis=1), (2, 1))
@@ -513,22 +607,20 @@
     )(near, courant_near, before, after)
 
     lines = NY // bricks
-    swapped = lax.all_to_all(
-        moments.reshape(2, 3, bricks, lines, lattice_z).transpose(2, 0, 1, 3, 4),
-        "dev",
-        split_axis=0,
-        concat_axis=0,
-        tiled=True,
-    )
     mine = lax.dynamic_slice_in_dim(factors[0], lax.axis_index("dev") * lines, lines)
-    solved = pl.pallas_call(
+    shared = (2, 3, bricks, lines, lattice_z)
+    edges = pl.pallas_call(
         functools.partial(reduced_kernel, planes),
-        out_shape=f32(swapped.shape),
+        out_shape=f32(shared),
         in_specs=[VMEM, VMEM],
         out_specs=VMEM,
-    )(swapped, mine)
-    edges = lax.all_to_all(solved, "dev", split_axis=0, concat_axis=0, tiled=True)
-    edges = edges.transpose(1, 2, 0, 3, 4).reshape(2, 3, NY, lattice_z)
+        scratch_shapes=[pltpu.VMEM(shared, jnp.float32)] * 2
+        + [pltpu.SemaphoreType.DMA((2, bricks))] * 2
+        + [pltpu.SemaphoreType.DMA],
+        compiler_params=pltpu.CompilerParams(
+            collective_id=2, has_side_effects=True, vmem_limit_bytes=32 * 1024 * 1024
+        ),
+    )(moments.reshape(shared), mine).reshape(2, 3, NY, lattice_z)
 
     fields, interp = pl.pallas_call(
         backward_kernel,
@@ -554,7 +646,7 @@
         advanced.reshape(3, slab_rows, lattice_z),
     )
 
-    returned, index_back = exchange(pack(interp, slot_back, 1), tags_back, 1)
+    returned, index_back = exchange(pack(interp, slots, 1), 1)
     fields = pl.pallas_call(
         functools.partial(finish_kernel, cap, stride, bricks),
         out_shape=f32((3, rows_j, NI, span_cells)),

time: 518 us -> 479 us (0.925)
  the two profiles are of different devices: /device:TPU:21 before, /device:TPU:29 now
where the time goes in v2:
time: 479 us
  Pallas kernels  462 us (96%)
  local copies, waits for them, and re-layouts  11.2 us (2%)
    pallas_call x2, Pallas kernels, exchange(): pl.pallas_call(functools.partial(exchange_kernel, group, bricks, bool(edg...  380 us
    pallas_call x1, Pallas kernels, on_device(): pl.pallas_call(advance_kernel, out_shape=f32((3, rows_j, NI, span_cells))...  25.8 us
    pallas_call x1, Pallas kernels, on_device(): pl.pallas_call(functools.partial(finish_kernel, cap, stride, bricks), out...  23.4 us
    pallas_call x2, Pallas kernels, pack(): pl.pallas_call(functools.partial(pack_kernel, cap, group), out_shape=f32(...  13.7 us
    pallas_call x1, Pallas kernels, on_device(): pl.pallas_call(functools.partial(index_kernel, cap, stride, bricks), out_...  12 us

profile of v2, /device:TPU:29, one launch (start us, length us, event | category | flops | bytes accessed | tf_op | source)
XLA Modules:
  0.0 479.4 jit_solution(9921506816651011464)
XLA Ops:
  0.0 0.0 copy-start.2
  0.0 1.3 broadcast_select_fusion
  1.3 1.3 broadcast_select_fusion.1.tag
  2.6 12.0 %shard_map.109 = (s32[2048]{0:T(1024)}, s32[6144]{0:T(1024)}) custom-call(s32[2048]{0:T(1024)} %bitcast.42, s32[2048]{0:T(1024)} %broadcast_select_fusion.1.tag), custom_call_target="tpu_custom_call" | custom-call | tf_op jit(solution)/shard_map/pallas_call | solution.py:539
  14.6 2.1 slice.12
  16.8 0.0 copy-done.2
  16.8 3.0 fusion.rows
  19.8 0.0 copy-start.3
  19.8 9.1 %shard_map.110 = f32[12288,128]{1,0:T(8,128)} custom-call(s32[2048]{0:T(1024)} %get-tuple-element.17.slot, f32[3,2048,128]{2,1,0:T(8,128)} %fusion.rows), custom_call_target="tpu_custom_call" | custom-call | tf_op jit(solution)/shard_map/pallas_call | solution.py:551
  28.9 0.0 copy-done.3
  28.9 0.6 reshape.47.refs_1_
  29.5 111.0 %shard_map.111 = (f32[16,768,128]{2,1,0:T(8,128)}, s32[16,3,128]{2,1,0:T(4,128)}, f32[4,4,64,128]{3,2,1,0:T(8,128)}, f32[4,4,64,128]{3,2,1,0:T(8,128)}) custom-call(f32[16,768,128]{2,1,0:T(8,128)} %bitcast.34, s32[16,3,128]{2,1,0:T(4,128)} %reshape.47.refs_1_, f32[3,128,64,128]{3,2,1,0:T(8,128)} %bitcast.27, f32[128,64,128]{2,1,0:T(8,128)} %bitcast.35), custom_call_target="tpu_custom_call" | custom-call | tf_op jit(solution)/shard_map/pallas_call | solution.py:562
  140.5 1.4 reshape.49.index
  141.9 3.8 shard_map.112
  145.7 0.7 dynamic-slice_bitcast_fusion.decay
  146.4 0.0 copy-start.1
  146.4 1.1 copy-done.1
  147.6 0.6 shard_map.113
  148.2 0.0 copy-start
  148.2 0.9 copy-done
  149.1 25.8 %shard_map.114 = f32[3,128,64,128]{3,2,1,0:T(8,128)} custom-call(f32[3,128,64,128]{3,2,1,0:T(8,128)} %bitcast.29, f32[128,64,128]{2,1,0:T(8,128)} %bitcast.36, f32[4,4,64,128]{3,2,1,0:T(8,128)} %get-tuple-element.23.before, f32[4,4,64,128]{3,2,1,0:T(8,128)} %get-tuple-element.24.after), custom_call_target="tpu_custom_call" | custom-call | tf_op jit(solution)/shard_map/pallas_call | solution.py:596
  174.8 0.7 copy.18
  175.5 3.0 shard_map.115
  178.6 4.6 shard_map.116
  183.1 269.2 %shard_map.117 = (f32[16,768,128]{2,1,0:T(8,128)}, s32[16,3,128]{2,1,0:T(4,128)}) custom-call(f32[16,768,128]{2,1,0:T(8,128)} %bitcast.33, s32[16,3,128]{2,1,0:T(4,128)} %reshape.47.refs_1_), custom_call_target="tpu_custom_call" | custom-call | tf_op jit(solution)/shard_map/pallas_call | solution.py:562
  452.3 1.4 reshape.55.index
  453.7 2.2 slice.13
  456.0 23.4 %shard_map.118 = f32[3,128,64,128]{3,2,1,0:T(8,128)} custom-call(s32[6144]{0:T(1024)} %reshape.55.index, f32[12288,128]{1,0:T(8,128)} %bitcast.39, f32[3,128,128]{2,1,0:T(8,128)} %bitcast.40, f32[3,128,64,128]{3,2,1,0:T(8,128)} %bitcast.32), custom_call_target="tpu_custom_call", output_to_operand_aliasing={{}: (3, {})} | custom-call | tf_op jit(solution)/shard_map/pallas_call | solution.py:650
Async XLA Ops:
  0.0 16.8 %copy-start.2 = (f32[128,128]{1,0:T(8,128)S(1)}, f32[128,128]{1,0:T(8,128)}, u32[]{:S(2)}) copy-start(f32[128,128]{1,0:T(8,128)} %param.13) | copy-start | bytes 196612
  19.8 9.1 %copy-start.3 = (s32[6144]{0:T(1024)S(1)}, s32[6144]{0:T(1024)}, u32[]{:S(2)}) copy-start(s32[6144]{0:T(1024)} %get-tuple-element.18) | copy-start | bytes 73732
  146.4 1.1 copy-start.1
  148.2 0.9 copy-start

commit v3 on v2

--- a/solution.py
+++ b/solution.py
@@ -91,8 +91,8 @@
     loop(count // width, several)
 
 
-def index_kernel(cap, stride, bricks, dest, tag, slot, out):
-    half = dest.shape[0] // 2
+def index_kernel(cap, stride, bricks, dest_a, tag_a, dest_b, tag_b, slot, out):
+    half = dest_a.shape[0] // 2
 
     def clear(b):
         for end in range(2):
@@ -100,7 +100,7 @@
 
     loop(bricks, clear)
 
-    def place(q):
+    def place(dest, tag, q):
         at = [q, q + half]
         brick = [dest[n] for n in at]
         label = [tag[n] for n in at]
@@ -112,7 +112,11 @@
             out[base[end] + rank] = label[end]
             slot[at[end]] = brick[end] * (3 * cap) + rank
 
-    unrolled(half, 8, place)
+    for group, sides in enumerate(((dest_a, tag_a), (dest_b, tag_b))):
+
+        @pl.when(lax.axis_index("grp") == group)
+        def _(sides=sides):
+            unrolled(half, 8, functools.partial(place, *sides))
 
 
 def exchange_kernel(source, bricks, halo, *refs):
@@ -211,18 +215,34 @@
         loop(bricks, finish)
 
 
-def pack_kernel(cap, group, slot, rows, out):
-    @pl.when(lax.axis_index("grp") == group)
-    def _():
-        def place(i):
-            first = pl.multiple_of(i * 8, 8)
-            slots = [slot[first + t] for t in range(8)]
+def pack_kernel(cap, slot, near, remesh, out, shell, sem):
+    rows_j = near.shape[1]
+    depth = shell.shape[2]
+
+    @pl.when(lax.axis_index("grp") == 0)
+    def _():
+        move(near.at[:, :, pl.ds(NI - depth, depth), :], shell, sem).wait()
+        weights = doubled(split(remesh[...]))
+        count = min(16, rows_j)
+
+        def project(i):
             for c in range(3):
-                tile = rows[c, pl.ds(first, 8), :]
-                for t in range(8):
-                    out[pl.ds(slots[t] + c * cap, 1), :] = tile[t : t + 1, :]
-
-        loop(rows.shape[1] // 8, place)
+                block = shell[c, pl.ds(i * count, count)]
+                block = block.reshape(count * depth, block.shape[2])
+                block = dot_doubled(block, weights)
+                shell[c, pl.ds(i * count, count)] = block.reshape(count, depth, block.shape[1])
+
+        loop(rows_j // count, project)
+
+        def place(j):
+            for half in range(depth // 8):
+                slots = [slot[j * depth + half * 8 + t] for t in range(8)]
+                for c in range(3):
+                    tile = shell[c, j, half * 8 : half * 8 + 8, :]
+                    for t in range(8):
+                        out[pl.ds(slots[t] + c * cap, 1), :] = tile[t : t + 1, :]
+
+        loop(rows_j, place)
 
 
 def accumulate(cap, stride, bricks, index, arrived, total):
@@ -372,7 +392,22 @@
 
 
 def backward_kernel(
-    row, spectral, edges, decay, table_y, table_z, remesh_t, _fields, fields, interp, held, pot, run, sem
+    cap,
+    row,
+    slot,
+    spectral,
+    edges,
+    decay,
+    table_y,
+    table_z,
+    remesh_t,
+    _fields,
+    fields,
+    packed,
+    held,
+    pot,
+    run,
+    sem,
 ):
     planes = spectral.shape[1] // NY
 
@@ -447,20 +482,21 @@
         def pick(i):
             first = pl.multiple_of(i * 8, 8)
             places = [row[first + t] for t in range(8)]
-            for c in range(3):
-                for t in range(8):
-                    interp[c, pl.ds(first + t, 1), :] = held[c, pl.ds(places[t], 1), :]
-
-        loop(interp.shape[1] // 8, pick)
+            slots = [slot[first + t] for t in range(8)]
+            for t in range(8):
+                picked = [held[c, pl.ds(places[t], 1), :] for c in range(3)]
+                for c in range(3):
+                    packed[pl.ds(slots[t] + c * cap, 1), :] = picked[c]
+
+        loop(row.shape[0] // 8, pick)
         weights = doubled(split(remesh_t[...]))
-        count = min(256, interp.shape[1])
+        count = 512 if packed.shape[0] % 512 == 0 else packed.shape[0]
 
         def project(i):
             rows = pl.ds(pl.multiple_of(i * count, count), count)
-            for c in range(3):
-                interp[c, rows, :] = dot_doubled(interp[c, rows, :], weights)
-
-        loop(interp.shape[1] // count, project)
+            packed[rows, :] = dot_doubled(packed[rows, :], weights)
+
+        loop(packed.shape[0] // count, project)
         sent.wait()
 
 
@@ -501,18 +537,23 @@
         move(ext.at[pl.ds(0, 3), pl.ds(0, rows_j)], out, sems.at[0]).wait()
 
 
-def finish_kernel(cap, stride, bricks, index, arrived, layer, _fields, fields, boundary, rim, sem):
+def finish_kernel(cap, stride, bricks, index, arrived, near, _fields, fields, boundary, rim, layer, sems):
     @pl.when(lax.axis_index("grp") == 0)
     def _():
-        fetched = move(fields.at[:, :, pl.ds(NI - 8, 8), :], rim, sem)
+        top = pl.ds(NI - 8, 8)
+        fetched = move(fields.at[:, :, top, :], rim, sems.at[0])
+        known = move(near.at[:, :, top, :], layer, sems.at[1])
         boundary[...] = jnp.zeros_like(boundary)
         accumulate(cap, stride, bricks, index, arrived, boundary)
         fetched.wait()
+        known.wait()
         for c in range(3):
             a, b = (c + 1) % 3, (c + 2) % 3
-            turned = coupling * (boundary[a] * layer[b] - boundary[b] * layer[a])
+            turned = coupling * (
+                boundary[a] * layer[b, :, 7, :] - boundary[b] * layer[a, :, 7, :]
+            )
             rim[c, :, 7, :] += turned
-        move(rim, fields.at[:, :, pl.ds(NI - 8, 8), :], sem).wait()
+        move(rim, fields.at[:, :, top, :], sems.at[0]).wait()
 
 
 def on_device(state, courant, remesh, shell_dest, shell_row, return_dest, return_row, return_block):
@@ -531,30 +572,26 @@
     field = state[0].reshape(3, slab_rows, lattice_z)
     near = field.reshape(3, rows_j, NI, span_cells)
 
-    blocks = near[:, :, NI - shell_depth :, :].reshape(3, shell_blocks, span_cells)
-    remeshed = jnp.einsum("cqk,kz->cqz", blocks, remesh, precision=lax.Precision.HIGH)
-
     courant_near = courant.reshape(rows_j, NI, span_cells)
-    on_near = lax.axis_index("grp") == 0
     slots, tags = pl.pallas_call(
         functools.partial(index_kernel, cap, stride, bricks),
         out_shape=(i32((shell_blocks,)), i32((bricks * stride,))),
-        in_specs=[SMEM] * 2,
+        in_specs=[SMEM] * 4,
         out_specs=(SMEM,) * 2,
-    )(
-        jnp.where(on_near, shell_dest[:, 0], return_dest[:, 0]),
-        jnp.where(on_near, shell_row, return_block),
-    )
+    )(shell_dest[:, 0], shell_row, return_dest[:, 0], return_block)
     tags = tags.reshape(bricks, stride // 128, 128)
 
-    def pack(rows, slots, group):
-        return pl.pallas_call(
-            functools.partial(pack_kernel, cap, group),
-            out_shape=f32((bricks * 3 * cap, lattice_z)),
-            in_specs=[SMEM, VMEM],
-            out_specs=VMEM,
-            compiler_params=ROOM,
-        )(slots, rows).reshape(bricks, 3 * cap, lattice_z)
+    packed_shell = pl.pallas_call(
+        functools.partial(pack_kernel, cap),
+        out_shape=f32((bricks * 3 * cap, lattice_z)),
+        in_specs=[SMEM, HBM, VMEM],
+        out_specs=VMEM,
+        scratch_shapes=[
+            pltpu.VMEM((3, rows_j, shell_depth, span_cells), jnp.float32),
+            pltpu.SemaphoreType.DMA,
+        ],
+        compiler_params=ROOM,
+    )(slots, near, remesh)
 
     def exchange(packed, group, *edge):
         rim = f32((4, 4, NI, span_cells))
@@ -571,10 +608,10 @@
             scratch_shapes=[pltpu.SemaphoreType.DMA((2, bricks))] * 2
             + [pltpu.SemaphoreType.DMA((4,))] * extra,
             compiler_params=pltpu.CompilerParams(collective_id=group, has_side_effects=True),
-        )(packed, tags, *edge)
+        )(packed.reshape(bricks, 3 * cap, lattice_z), tags, *edge)
         return arrived.reshape(bricks * 3 * cap, lattice_z), index.reshape(-1), *rims
 
-    arrived, index, before, after = exchange(pack(remeshed, slots, 0), 0, near, courant_near)
+    arrived, index, before, after = exchange(packed_shell, 0, near, courant_near)
 
     table_y = sine_table(NY)
     table_z = np.tile(np.concatenate(list(sine_table(lattice_z)), axis=1), (2, 1))
@@ -622,10 +659,10 @@
         ),
     )(moments.reshape(shared), mine).reshape(2, 3, NY, lattice_z)
 
-    fields, interp = pl.pallas_call(
-        backward_kernel,
-        out_shape=(f32((3, slab_rows, lattice_z)), f32((3, shell_blocks, span_cells))),
-        in_specs=[SMEM, HBM, VMEM, VMEM, VMEM, VMEM, VMEM, HBM],
+    fields, packed_back = pl.pallas_call(
+        functools.partial(backward_kernel, cap),
+        out_shape=(f32((3, slab_rows, lattice_z)), f32((bricks * 3 * cap, span_cells))),
+        in_specs=[SMEM, SMEM, HBM, VMEM, VMEM, VMEM, VMEM, VMEM, HBM],
         out_specs=(HBM, VMEM),
         scratch_shapes=[
             pltpu.VMEM((3, slab_rows, lattice_z), jnp.float32),
@@ -633,10 +670,11 @@
             pltpu.VMEM((2, 3, NY, lattice_z), jnp.float32),
             pltpu.SemaphoreType.DMA,
         ],
-        input_output_aliases={7: 0},
+        input_output_aliases={8: 0},
         compiler_params=ROOM,
     )(
         return_row,
+        slots,
         spectral,
         edges,
         factors,
@@ -646,20 +684,21 @@
         advanced.reshape(3, slab_rows, lattice_z),
     )
 
-    returned, index_back = exchange(pack(interp, slots, 1), 1)
+    returned, index_back = exchange(packed_back, 1)
     fields = pl.pallas_call(
         functools.partial(finish_kernel, cap, stride, bricks),
         out_shape=f32((3, rows_j, NI, span_cells)),
-        in_specs=[SMEM, VMEM, VMEM, HBM],
+        in_specs=[SMEM, VMEM, HBM, HBM],
         out_specs=HBM,
         scratch_shapes=[
             pltpu.VMEM((3, rows_j, span_cells), jnp.float32),
             pltpu.VMEM((3, rows_j, 8, span_cells), jnp.float32),
-            pltpu.SemaphoreType.DMA,
+            pltpu.VMEM((3, rows_j, 8, span_cells), jnp.float32),
+            pltpu.SemaphoreType.DMA((2,)),
         ],
         input_output_aliases={3: 0},
         compiler_params=ROOM,
-    )(index_back, returned, near[:, :, NI - 1, :], fields.reshape(3, rows_j, NI, span_cells))
+    )(index_back, returned, near, fields.reshape(3, rows_j, NI, span_cells))
     return fields.reshape(1, 3, cell_count)
 
 

time: 479 us -> 463 us (0.967)
  the two profiles are of different devices: /device:TPU:29 before, /device:TPU:21 now
where the time goes in v3:
time: 463 us; the launch traced here: 461 us
  Pallas kernels  452 us (98%)
  local copies, waits for them, and re-layouts  8.38 us (2%)
    pallas_call x2, Pallas kernels, exchange(): pl.pallas_call(functools.partial(exchange_kernel, group, bricks, bool(edg...  378 us
    pallas_call x1, Pallas kernels, on_device(): pl.pallas_call(advance_kernel, out_shape=f32((3, rows_j, NI, span_cells))...  25.8 us
    pallas_call x1, Pallas kernels, on_device(): pl.pallas_call(functools.partial(finish_kernel, cap, stride, bricks), out...  15.9 us
    pallas_call x1, Pallas kernels, on_device(): pl.pallas_call(functools.partial(index_kernel, cap, stride, bricks), out_...  12.3 us
    pallas_call x1, Pallas kernels, on_device(): pl.pallas_call(functools.partial(pack_kernel, cap), out_shape=f32((bricks...  11.5 us

profile of v3, /device:TPU:21, one launch (start us, length us, event | category | flops | bytes accessed | tf_op | source)
XLA Modules:
  0.0 460.6 jit_solution(16194303171458607882)
XLA Ops:
  0.0 0.7 dynamic-slice_bitcast_fusion.decay
  0.7 12.3 %shard_map.109 = (s32[2048]{0:T(1024)}, s32[6144]{0:T(1024)}) custom-call(s32[2048]{0:T(1024)} %bitcast.33, s32[2048]{0:T(1024)} %tag_a.1, s32[2048]{0:T(1024)} %bitcast.34, s32[2048]{0:T(1024)} %tag_b.1), custom_call_target="tpu_custom_call" | custom-call | tf_op jit(solution)/shard_map/pallas_call | solution.py:576
  13.0 1.4 reshape.41.refs_1_
  14.4 1.6 copy.16
  15.9 11.5 %shard_map.110 = f32[12288,128]{1,0:T(8,128)} custom-call(s32[2048]{0:T(1024)} %get-tuple-element.17.slot, f32[3,128,64,128]{3,2,1,0:T(8,128)} %bitcast.19, f32[128,128]{1,0:T(8,128)} %remesh.1), custom_call_target="tpu_custom_call" | custom-call | tf_op jit(solution)/shard_map/pallas_call | solution.py:584
  27.5 143.9 %shard_map.111 = (f32[16,768,128]{2,1,0:T(8,128)}, s32[16,3,128]{2,1,0:T(4,128)}, f32[4,4,64,128]{3,2,1,0:T(8,128)}, f32[4,4,64,128]{3,2,1,0:T(8,128)}) custom-call(f32[16,768,128]{2,1,0:T(8,128)} %bitcast.26, s32[16,3,128]{2,1,0:T(4,128)} %reshape.41.refs_1_, f32[3,128,64,128]{3,2,1,0:T(8,128)} %bitcast.20, f32[128,64,128]{2,1,0:T(8,128)} %bitcast.27), custom_call_target="tpu_custom_call" | custom-call | tf_op jit(solution)/shard_map/pallas_call | solution.py:599
  171.4 1.4 reshape.43.index
  172.7 3.8 shard_map.112
  176.5 0.0 copy-start.1
  176.5 1.1 copy-done.1
  177.7 0.6 shard_map.113
  178.3 0.0 copy-start
  178.3 0.9 copy-done
  179.2 25.8 %shard_map.114 = f32[3,128,64,128]{3,2,1,0:T(8,128)} custom-call(f32[3,128,64,128]{3,2,1,0:T(8,128)} %bitcast.22, f32[128,64,128]{2,1,0:T(8,128)} %bitcast.28, f32[4,4,64,128]{3,2,1,0:T(8,128)} %get-tuple-element.23.before, f32[4,4,64,128]{3,2,1,0:T(8,128)} %get-tuple-element.24.after), custom_call_target="tpu_custom_call" | custom-call | tf_op jit(solution)/shard_map/pallas_call | solution.py:633
  204.9 4.0 shard_map.115
  208.9 234.4 %shard_map.116 = (f32[16,768,128]{2,1,0:T(8,128)}, s32[16,3,128]{2,1,0:T(4,128)}) custom-call(f32[16,768,128]{2,1,0:T(8,128)} %bitcast.30, s32[16,3,128]{2,1,0:T(4,128)} %reshape.41.refs_1_), custom_call_target="tpu_custom_call" | custom-call | tf_op jit(solution)/shard_map/pallas_call | solution.py:599
  443.3 1.4 reshape.49.index
  444.7 15.9 %shard_map.117 = f32[3,128,64,128]{3,2,1,0:T(8,128)} custom-call(s32[6144]{0:T(1024)} %reshape.49.index, f32[12288,128]{1,0:T(8,128)} %bitcast.31, f32[3,128,64,128]{3,2,1,0:T(8,128)} %bitcast.23, f32[3,128,64,128]{3,2,1,0:T(8,128)} %bitcast.25), custom_call_target="tpu_custom_call", output_to_operand_aliasing={{}: (3, {})} | custom-call | tf_op jit(solution)/shard_map/pallas_call | solution.py:688
Async XLA Ops:
  176.5 1.1 copy-start.1
  178.3 0.9 copy-start
